TPU v7x, 256 devices: a whole 4x4x8 slice. The times are simulated.
256 devices in a mesh: queue: 8 (over x, core), seq: 32 (over z, y).
Axes of the slice: x: 4, y: 4, z: 8, core: 2. Of those that a mesh axis runs over, the one named last changes fastest.
Arguments:
- hidden: bfloat16 [8, 1536, 3072], P('queue', 'seq'), may hold values from -1.1953125 to 1.1953125
- queries: bfloat16 [8, 1536, 2048], P('queue', 'seq'), may hold values from -64 to 64
- keys: bfloat16 [8, 1536, 2048], P('queue', 'seq'), may hold values from -30 to 30
- values: bfloat16 [8, 1536, 2048], P('queue', 'seq'), may hold values from -6 to 6
- timesteps: int32 [8], P('queue'), may hold values from 125 to 1000, as said below
- latents: float32 [8, 1536, 64], P('queue', 'seq'), may hold values from -6 to 6
- fresh_noise: float32 [1536, 64], P('seq'), may hold values from -6 to 6
- out_weight: bfloat16 [2048, 3072], P('seq'), may hold values from -0.125 to 0.125
- mod_weight: bfloat16 [256, 9216], replicated, may hold values from -0.75 to 0.75
- final_weight: bfloat16 [3072, 64], replicated, may hold values from -0.109375 to 0.109375
Outputs:
- velocity: float32 [8, 1536, 64], P('queue', 'seq')
- next_latents: float32 [8, 1536, 64], P('queue', 'seq')
Inputs may be any that keep to these rules, and one draw needn't show every extreme that they name: timesteps fall strictly along the queue: the first block's is 1000 and the last block's is 125.
All inputs are finite; a program needn't handle non-finite values.
Results may differ from a plain program's by a relative error of at most 0.008.
Values may be sent and summed in bfloat16 or wider, within the bound.
A program may use at most 128 MiB of HBM per device.

v0:
```python
import math

import jax
import jax.numpy as jnp
from jax import lax
from jax.sharding import PartitionSpec as P

D = 3072
H = 16
DH = 128
TEMB = 256
STRIDE = 125


def from_behind(array, axis, by):
    count = lax.axis_size(axis)
    pairs = [(i, i + by) for i in range(count) if 0 <= i + by < count]
    return lax.ppermute(array, axis, pairs)


def time_embed(step_values):
    halfway = TEMB // 2
    freqs = jnp.exp(-math.log(10000.0) * jnp.arange(halfway, dtype=jnp.float32) / halfway)
    angles = step_values.astype(jnp.float32)[:, None] * freqs[None, :]
    return jnp.concatenate([jnp.cos(angles), jnp.sin(angles)], axis=1)


def fold_block(carry, query_heads, key_block, first_row, group, block_rows, queue_count):
    running_peak, running_total, numerator = carry
    per_device = query_heads.shape[1]
    row_count = key_block.shape[1]
    key_part = key_block[0].reshape(row_count, per_device, DH)
    value_part = key_block[1].reshape(row_count, per_device, DH)
    scores = jnp.einsum(
        "qhd,khd->hqk", query_heads, key_part, preferred_element_type=jnp.float32
    ) * DH ** (-0.5)
    owner = (first_row + jnp.arange(row_count, dtype=jnp.int32)) // block_rows
    visible = ((owner >= group) & (owner < queue_count))[None, None, :]
    masked = jnp.where(visible, scores, -1e30)
    new_peak = jnp.maximum(running_peak, jnp.max(masked, axis=2))
    weights = jnp.where(visible, jnp.exp(scores - new_peak[..., None]), 0.0)
    factor = jnp.exp(running_peak - new_peak)
    new_total = running_total * factor + jnp.sum(weights, axis=2)
    mixed = jnp.einsum(
        "hqk,khd->hqd", weights.astype(jnp.bfloat16), value_part, preferred_element_type=jnp.float32
    )
    new_numerator = numerator * factor[..., None] + mixed
    return (new_peak, new_total, new_numerator)


def fold_rows(carry, piece, query_heads, group, block_rows, queue_count):
    row_count = piece.shape[1]
    step_rows = math.gcd(row_count, 2048)

    def advance(index, inner):
        sliced = lax.dynamic_slice_in_dim(piece, index * step_rows, step_rows, 1)
        return fold_block(
            inner, query_heads, sliced, index * step_rows, group, block_rows, queue_count
        )

    return lax.fori_loop(0, row_count // step_rows, advance, carry)


def body(
    hidden,
    queries,
    keys,
    values,
    timesteps,
    latents,
    fresh_noise,
    out_weight,
    mod_weight,
    final_weight,
):
    seq_count = lax.axis_size("seq")
    queue_count = lax.axis_size("queue")
    group = lax.axis_index("queue")
    tok_rows = hidden.shape[1]
    per_device = max(H // seq_count, 1)
    query_split = max(seq_count // H, 1)
    head_groups = H // per_device
    head_width = per_device * DH
    half_rows = tok_rows // query_split
    query_send = queries[0].reshape(query_split, half_rows, head_groups, head_width)
    query_send = query_send.transpose(2, 0, 1, 3).reshape(1, seq_count, half_rows, head_width)
    paired = jnp.stack([keys[0], values[0]]).reshape(2, tok_rows, head_groups, 1, head_width)
    paired = jnp.broadcast_to(paired, (2, tok_rows, head_groups, query_split, head_width))
    paired = paired.transpose(0, 2, 3, 1, 4).reshape(2, seq_count, tok_rows, head_width)
    query_in, pair_in = (
        lax.all_to_all(query_send, "seq", split_axis=1, concat_axis=2, tiled=True),
        lax.all_to_all(paired, "seq", split_axis=1, concat_axis=2, tiled=True),
    )
    query_heads = query_in.reshape(-1, per_device, DH)
    own_pairs = pair_in.reshape(2, -1, head_width)
    block_rows = own_pairs.shape[1]
    query_rows = query_heads.shape[0]
    start_state = (
        jnp.full((per_device, query_rows), -1e30, jnp.float32),
        jnp.zeros((per_device, query_rows), jnp.float32),
        jnp.zeros((per_device, query_rows, DH), jnp.float32),
    )
    final_state = fold_rows(
        start_state,
        lax.all_gather(own_pairs, "queue", axis=1, tiled=True),
        query_heads,
        group,
        block_rows,
        queue_count,
    )
    attended = (final_state[2] / final_state[1][..., None]).astype(jnp.bfloat16)
    attended = attended.transpose(1, 0, 2).reshape(seq_count, half_rows, 1, head_width)
    returned = lax.all_to_all(attended, "seq", split_axis=0, concat_axis=2, tiled=True)
    returned = returned.reshape(half_rows, head_groups, query_split, head_width)
    attn_rows = returned.transpose(2, 0, 1, 3).reshape(tok_rows, H * DH)
    projected = jnp.dot(
        attn_rows,
        lax.all_gather(out_weight, "seq", axis=0, tiled=True),
        preferred_element_type=jnp.float32,
    )
    embed = time_embed(timesteps)
    activated = jax.nn.silu(embed).astype(jnp.bfloat16)
    modulation = jnp.dot(activated, mod_weight, preferred_element_type=jnp.float32)[0]
    gate = modulation[:D]
    shift_vec = modulation[D : 2 * D]
    scale_vec = modulation[2 * D :]
    stream = hidden[0].astype(jnp.float32) + gate[None, :] * projected
    center = jnp.mean(stream, axis=1, keepdims=True)
    spread = jnp.mean((stream - center) ** 2, axis=1, keepdims=True)
    normed = (stream - center) / jnp.sqrt(spread + 1e-06) * (1.0 + scale_vec[None, :]) + shift_vec[
        None, :
    ]
    normed = normed.astype(jnp.bfloat16)
    velocity = jnp.dot(normed, final_weight, preferred_element_type=jnp.float32)
    updated = latents[0] - STRIDE / 1000.0 * velocity
    moved = from_behind(updated, "queue", 1)
    next_block = jnp.where(group == 0, fresh_noise, moved)
    return (velocity[None], next_block[None])


def solution(mesh):
    placed = (
        P("queue", "seq", None),
        P("queue", "seq", None),
        P("queue", "seq", None),
        P("queue", "seq", None),
        P("queue"),
        P("queue", "seq", None),
        P("seq", None),
        P("seq", None),
        P(),
        P(),
    )
    return jax.shard_map(
        body,
        mesh=mesh,
        in_specs=placed,
        out_specs=(P("queue", "seq", None), P("queue", "seq", None)),
        check_vma=False,
    )
```

profile of v0, /device:TPU:7, one launch (start us, length us, event | category | flops | bytes accessed | tf_op | source)
XLA Modules:
  0.0 229.4 jit_solution(10515060887358747798)
XLA Ops:
  7.2 0.0 copy-start
  7.2 0.0 copy-start.3
  7.2 0.0 all-gather.3.cloned.1.call-start
  7.2 1.2 copy_bitcast_fusion
  8.4 0.1 broadcast_in_dim.71
  8.5 32.1 %all_to_all.33 = bf16[2,32,48,128]{3,2,0,1:T(8,128)(2,1)S(1)} all-to-all(bf16[2,32,48,128]{3,2,0,1:T(8,128)(2,1)S(1)} %bitcast.73), channel_id=1, replica_groups=mesh['queue'=8,'seq'=32] {'seq'}, dimensions={1} | all-to-all | bytes 1572864 | tf_op jit(solution)/shard_map/all_to_all | solution.py:92
  40.6 1.0 copy.23
  41.6 0.0 all-gather.3.cloned.1.call-update
  41.6 0.0 all-gather.5.cloned.1.call-start
  41.7 0.7 all-gather.5.cloned.1.call-update
  42.4 0.0 copy-done.3
  42.4 0.7 copy.24
  43.1 5.8 %all-to-all-start.1 = ((bf16[1,32,24,128]{3,2,0,1:T(8,128)(2,1)}), bf16[1,32,24,128]{3,2,0,1:T(8,128)(2,1)S(1)}, u32[]{:S(2)}, u32[]{:S(2)}) async-start(bf16[1,32,24,128]{3,2,0,1:T(8,128)(2,1)} %bitcast.7), calls=%async_computation.1 | async-start | bytes 393216 | tf_op jit(solution)/shard_map/all_to_all | solution.py:91
  49.7 9.1 %all-to-all-done.1 = bf16[1,32,24,128]{3,2,0,1:T(8,128)(2,1)S(1)} async-done(((bf16[1,32,24,128]{3,2,0,1:T(8,128)(2,1)}), bf16[1,32,24,128]{3,2,0,1:T(8,128)(2,1)S(1)}, u32[]{:S(2)}, u32[]{:S(2)}) %all-to-all-start.1) | async-done | bytes 196640 | tf_op jit(solution)/shard_map/all_to_all | solution.py:91
  58.8 23.6 %all-gather.3.cloned.1.call-done = bf16[2,12288,128]{2,1,0:T(8,128)(2,1)} async-done(((bf16[2,1536,128]{2,1,0:T(8,128)(2,1)}), bf16[2,12288,128]{2,1,0:T(8,128)(2,1)}) %all-gather.3.cloned.1.call-update) | async-done | bytes 6291472 | tf_op jit(solution)/shard_map/all_gather | solution.py:105
  82.4 66.8 %while.20 = (s32[]{:T(128)}, f32[1,768]{1,0:T(1,128)S(1)}, f32[1,768]{1,0:T(1,128)S(1)}, f32[1,768,128]{2,1,0:T(8,128)S(1)}, s32[]{:T(128)}, /*index=5*/bf16[2,1...) while((s32[]{:T(128)}, f32[1,768]{1,0:T(1,128)S(1)}, ...), condition=%wide.region_3.4_spmd.clone, body=%wide.region_0.3_spmd.clone.sunk | while | flops 822931968 | bytes 46132456 | solution.py:61
  82.4 4.7 %select_reduce_fusion.2 = (f32[768]{0:T(1024)S(1)}, f32[2048,768]{1,0:T(8,128)}) fusion(pred[2048]{0:T(1024)(128)(4,1)S(1)} %compare_and_fusion.2, bf16[768,1,128]{2,0,1:T(8,128)(2,1)S(1)} %get-tuple-element.317, bf16[2,12288,128]{2,1,0:T(8,128)(2,1)} %get-tuple-element.316, s32[]{:T(128)S(6)} %select_n.92), kind=kOutput, calls=%fused_computation.1.clone.1 | convolution fusion | flops 407371008 | bytes 7017476 | tf_op jit(solution)/shard_map/while/body/eval_jaxpr/qhd,khd->hqk/dot_general | solution.py:34
  87.2 0.0 copy-start.1
  87.2 4.9 %fusion.43 = f32[1,768,128]{2,1,0:T(8,128)S(1)} fusion(f32[2048,768]{1,0:T(8,128)} %get-tuple-element.284, f32[768]{0:T(1024)S(1)} %get-tuple-element.285, pred[2048]{0:T(1024)(128)(4,1)S(1)} %compare_and_fusion.2, bf16[2,12288,128]{2,1,0:T(8,128)(2,1)} %get-tuple-element.316, s32[]{:T(128)S(6)} %add.180, s32[]{:T(128)S(6)} %select_n.92, ...), kind=kOutput, calls=%fused_computation.7.clone.1 | convolution fusion | flops 409239552 | bytes 7610377 | tf_op jit(solution)/shard_map/while/body/eval_jaxpr/hqk,khd->hqd/dot_general | solution.py:44
  92.1 0.0 copy-done.1
  92.1 1.3 fusion.41
  93.5 4.7 %select_reduce_fusion.2 = (f32[768]{0:T(1024)S(1)}, f32[2048,768]{1,0:T(8,128)}) fusion(pred[2048]{0:T(1024)(128)(4,1)S(1)} %compare_and_fusion.2, bf16[768,1,128]{2,0,1:T(8,128)(2,1)S(1)} %get-tuple-element.317, bf16[2,12288,128]{2,1,0:T(8,128)(2,1)} %get-tuple-element.316, s32[]{:T(128)S(6)} %select_n.92), kind=kOutput, calls=%fused_computation.1.clone.1 | convolution fusion | flops 407371008 | bytes 7017476 | tf_op jit(solution)/shard_map/while/body/eval_jaxpr/qhd,khd->hqk/dot_general | solution.py:34
  98.2 0.0 copy-start.1
  98.3 5.2 %fusion.43 = f32[1,768,128]{2,1,0:T(8,128)S(1)} fusion(f32[2048,768]{1,0:T(8,128)} %get-tuple-element.284, f32[768]{0:T(1024)S(1)} %get-tuple-element.285, pred[2048]{0:T(1024)(128)(4,1)S(1)} %compare_and_fusion.2, bf16[2,12288,128]{2,1,0:T(8,128)(2,1)} %get-tuple-element.316, s32[]{:T(128)S(6)} %add.180, s32[]{:T(128)S(6)} %select_n.92, ...), kind=kOutput, calls=%fused_computation.7.clone.1 | convolution fusion | flops 409239552 | bytes 7610377 | tf_op jit(solution)/shard_map/while/body/eval_jaxpr/hqk,khd->hqd/dot_general | solution.py:44
  103.5 0.0 copy-done.1
  103.5 1.3 fusion.41
  104.9 4.7 %select_reduce_fusion.2 = (f32[768]{0:T(1024)S(1)}, f32[2048,768]{1,0:T(8,128)}) fusion(pred[2048]{0:T(1024)(128)(4,1)S(1)} %compare_and_fusion.2, bf16[768,1,128]{2,0,1:T(8,128)(2,1)S(1)} %get-tuple-element.317, bf16[2,12288,128]{2,1,0:T(8,128)(2,1)} %get-tuple-element.316, s32[]{:T(128)S(6)} %select_n.92), kind=kOutput, calls=%fused_computation.1.clone.1 | convolution fusion | flops 407371008 | bytes 7017476 | tf_op jit(solution)/shard_map/while/body/eval_jaxpr/qhd,khd->hqk/dot_general | solution.py:34
  109.6 0.0 copy-start.1
  109.7 5.0 %fusion.43 = f32[1,768,128]{2,1,0:T(8,128)S(1)} fusion(f32[2048,768]{1,0:T(8,128)} %get-tuple-element.284, f32[768]{0:T(1024)S(1)} %get-tuple-element.285, pred[2048]{0:T(1024)(128)(4,1)S(1)} %compare_and_fusion.2, bf16[2,12288,128]{2,1,0:T(8,128)(2,1)} %get-tuple-element.316, s32[]{:T(128)S(6)} %add.180, s32[]{:T(128)S(6)} %select_n.92, ...), kind=kOutput, calls=%fused_computation.7.clone.1 | convolution fusion | flops 409239552 | bytes 7610377 | tf_op jit(solution)/shard_map/while/body/eval_jaxpr/hqk,khd->hqd/dot_general | solution.py:44
  114.6 0.0 copy-done.1
  114.7 1.3 fusion.41
  116.1 4.7 %select_reduce_fusion.2 = (f32[768]{0:T(1024)S(1)}, f32[2048,768]{1,0:T(8,128)}) fusion(pred[2048]{0:T(1024)(128)(4,1)S(1)} %compare_and_fusion.2, bf16[768,1,128]{2,0,1:T(8,128)(2,1)S(1)} %get-tuple-element.317, bf16[2,12288,128]{2,1,0:T(8,128)(2,1)} %get-tuple-element.316, s32[]{:T(128)S(6)} %select_n.92), kind=kOutput, calls=%fused_computation.1.clone.1 | convolution fusion | flops 407371008 | bytes 7017476 | tf_op jit(solution)/shard_map/while/body/eval_jaxpr/qhd,khd->hqk/dot_general | solution.py:34
  120.8 0.0 copy-start.1
  120.8 4.9 %fusion.43 = f32[1,768,128]{2,1,0:T(8,128)S(1)} fusion(f32[2048,768]{1,0:T(8,128)} %get-tuple-element.284, f32[768]{0:T(1024)S(1)} %get-tuple-element.285, pred[2048]{0:T(1024)(128)(4,1)S(1)} %compare_and_fusion.2, bf16[2,12288,128]{2,1,0:T(8,128)(2,1)} %get-tuple-element.316, s32[]{:T(128)S(6)} %add.180, s32[]{:T(128)S(6)} %select_n.92, ...), kind=kOutput, calls=%fused_computation.7.clone.1 | convolution fusion | flops 409239552 | bytes 7610377 | tf_op jit(solution)/shard_map/while/body/eval_jaxpr/hqk,khd->hqd/dot_general | solution.py:44
  125.8 0.0 copy-done.1
  125.8 1.3 fusion.41
  127.2 4.7 %select_reduce_fusion.2 = (f32[768]{0:T(1024)S(1)}, f32[2048,768]{1,0:T(8,128)}) fusion(pred[2048]{0:T(1024)(128)(4,1)S(1)} %compare_and_fusion.2, bf16[768,1,128]{2,0,1:T(8,128)(2,1)S(1)} %get-tuple-element.317, bf16[2,12288,128]{2,1,0:T(8,128)(2,1)} %get-tuple-element.316, s32[]{:T(128)S(6)} %select_n.92), kind=kOutput, calls=%fused_computation.1.clone.1 | convolution fusion | flops 407371008 | bytes 7017476 | tf_op jit(solution)/shard_map/while/body/eval_jaxpr/qhd,khd->hqk/dot_general | solution.py:34
  131.9 0.0 copy-start.1
  131.9 4.9 %fusion.43 = f32[1,768,128]{2,1,0:T(8,128)S(1)} fusion(f32[2048,768]{1,0:T(8,128)} %get-tuple-element.284, f32[768]{0:T(1024)S(1)} %get-tuple-element.285, pred[2048]{0:T(1024)(128)(4,1)S(1)} %compare_and_fusion.2, bf16[2,12288,128]{2,1,0:T(8,128)(2,1)} %get-tuple-element.316, s32[]{:T(128)S(6)} %add.180, s32[]{:T(128)S(6)} %select_n.92, ...), kind=kOutput, calls=%fused_computation.7.clone.1 | convolution fusion | flops 409239552 | bytes 7610377 | tf_op jit(solution)/shard_map/while/body/eval_jaxpr/hqk,khd->hqd/dot_general | solution.py:44
  136.8 0.0 copy-done.1
  136.8 1.3 fusion.41
  138.3 4.7 %select_reduce_fusion.2 = (f32[768]{0:T(1024)S(1)}, f32[2048,768]{1,0:T(8,128)}) fusion(pred[2048]{0:T(1024)(128)(4,1)S(1)} %compare_and_fusion.2, bf16[768,1,128]{2,0,1:T(8,128)(2,1)S(1)} %get-tuple-element.317, bf16[2,12288,128]{2,1,0:T(8,128)(2,1)} %get-tuple-element.316, s32[]{:T(128)S(6)} %select_n.92), kind=kOutput, calls=%fused_computation.1.clone.1 | convolution fusion | flops 407371008 | bytes 7017476 | tf_op jit(solution)/shard_map/while/body/eval_jaxpr/qhd,khd->hqk/dot_general | solution.py:34
  143.0 0.0 copy-start.1
  143.0 4.9 %fusion.43 = f32[1,768,128]{2,1,0:T(8,128)S(1)} fusion(f32[2048,768]{1,0:T(8,128)} %get-tuple-element.284, f32[768]{0:T(1024)S(1)} %get-tuple-element.285, pred[2048]{0:T(1024)(128)(4,1)S(1)} %compare_and_fusion.2, bf16[2,12288,128]{2,1,0:T(8,128)(2,1)} %get-tuple-element.316, s32[]{:T(128)S(6)} %add.180, s32[]{:T(128)S(6)} %select_n.92, ...), kind=kOutput, calls=%fused_computation.7.clone.1 | convolution fusion | flops 409239552 | bytes 7610377 | tf_op jit(solution)/shard_map/while/body/eval_jaxpr/hqk,khd->hqd/dot_general | solution.py:44
  147.9 0.0 copy-done.1
  147.9 1.3 fusion.41
  149.3 0.0 copy-start.2
  149.3 0.9 divide_convert_fusion
  150.2 9.5 %all-to-all-start.2 = ((bf16[32,24,1,128]{3,1,2,0:T(8,128)(2,1)}), bf16[32,24,1,128]{3,1,2,0:T(8,128)(2,1)S(1)}, u32[]{:S(2)}, u32[]{:S(2)}) async-start(bf16[32,24,1,128]{3,1,2,0:T(8,128)(2,1)} %bitcast.9), calls=%async_computation.2 | async-start | bytes 393216 | tf_op jit(solution)/shard_map/all_to_all | solution.py:113
  159.7 3.3 %fusion.29 = f32[1,9216]{1,0:T(1,128)S(1)} fusion(bf16[256,1]{0,1:T(2,128)(2,1)S(1)} %reshape.188, bf16[256,9216]{1,0:T(8,128)(2,1)} %param.20), kind=kOutput, calls=%fused_computation.52 | convolution fusion | flops 4718592 | bytes 4755968 | tf_op jit(solution)/shard_map/dot_general | solution.py:123
  163.0 9.4 %all-to-all-done.2 = bf16[32,24,1,128]{3,1,2,0:T(8,128)(2,1)S(1)} async-done(((bf16[32,24,1,128]{3,1,2,0:T(8,128)(2,1)}), bf16[32,24,1,128]{3,1,2,0:T(8,128)(2,1)S(1)}, u32[]{:S(2)}, u32[]{:S(2)}) %all-to-all-start.2) | async-done | bytes 196640 | tf_op jit(solution)/shard_map/all_to_all | solution.py:113
  172.4 0.1 copy.25
  172.5 37.8 %all-gather.5.cloned.1.call-done = bf16[2048,3072]{1,0:T(8,128)(2,1)} async-done(((bf16[64,3072]{1,0:T(8,128)(2,1)}), bf16[2048,3072]{1,0:T(8,128)(2,1)}) %all-gather.5.cloned.1.call-update) | async-done | bytes 12582928 | tf_op jit(solution)/shard_map/all_gather | solution.py:118
  210.3 0.0 copy-done.2
  210.3 0.0 copy-start.5
  210.3 7.0 %fusion.28 = (f32[48]{0:T(128)S(1)}, f32[48,3072]{1,0:T(8,128)S(1)}) fusion(bf16[2048,3072]{1,0:T(8,128)(2,1)} %all-gather.5.cloned.1.call-done, bf16[6,8,16,128]{3,2,1,0:T(8,128)(2,1)S(1)} %bitcast.74, f32[3072]{0:T(1024)S(1)} %get-tuple-element.227, bf16[1,48,3072]{2,1,0:T(8,128)(2,1)S(1)} %copy-done.2), kind=kOutput, calls=%fused_computation.51 | convolution fusion | flops 604569536 | bytes 13676736 | tf_op jit(solution)/shard_map/dot_general | solution.py:116
  217.3 0.2 multiply_reduce_fusion
  217.5 0.0 copy-done
  217.5 0.0 copy-done.5
  217.6 0.9 bitcast_subtract_fusion
  218.5 1.3 collective-permute-start
  219.8 2.1 collective-permute-done
  221.9 0.0 copy-done.4
  221.9 0.6 select_bitcast_fusion
  (36 shorter events, 0.5 us)
Async XLA Ops:
  7.2 210.4 %copy-start = (bf16[3072,64]{0,1:T(8,128)(2,1)S(1)}, bf16[3072,64]{0,1:T(8,128)(2,1)}, u32[]{:S(2)}) copy-start(bf16[3072,64]{0,1:T(8,128)(2,1)} %param.21) | copy-start | bytes 1179652
  7.2 35.2 %copy-start.3 = (bf16[1,48,2048]{2,1,0:T(8,128)(2,1)S(1)}, bf16[1,48,2048]{2,1,0:T(8,128)(2,1)}, u32[]{:S(2)}) copy-start(bf16[1,48,2048]{2,1,0:T(8,128)(2,1)} %param.13) | copy-start | bytes 589828
  7.2 75.2 %all-gather.3.cloned.1.call-start = ((), (), s32[]{:S(2)}) async-start(), calls=%async_computation.3 | async-start | bytes 7077888 | tf_op jit(solution)/shard_map/all_gather | solution.py:105
  41.6 168.7 %all-gather.5.cloned.1.call-start = ((), (), s32[]{:S(2)}) async-start(), calls=%async_computation.4 | async-start | bytes 12976128 | tf_op jit(solution)/shard_map/all_gather | solution.py:118
  43.1 15.6 %all-to-all-start.1 = ((bf16[1,32,24,128]{3,2,0,1:T(8,128)(2,1)}), bf16[1,32,24,128]{3,2,0,1:T(8,128)(2,1)S(1)}, u32[]{:S(2)}, u32[]{:S(2)}) async-start(bf16[1,32,24,128]{3,2,0,1:T(8,128)(2,1)} %bitcast.7), calls=%async_computation.1 | async-start | bytes 393216 | tf_op jit(solution)/shard_map/all_to_all | solution.py:91
  87.2 4.9 %copy-start.1 = (f32[2048,768]{1,0:T(8,128)S(1)}, f32[2048,768]{1,0:T(8,128)}, u32[]{:S(2)}) copy-start(f32[2048,768]{1,0:T(8,128)} %get-tuple-element.284) | copy-start | bytes 18874372 | tf_op jit(solution)/shard_map/while
  98.2 5.2 %copy-start.1 = (f32[2048,768]{1,0:T(8,128)S(1)}, f32[2048,768]{1,0:T(8,128)}, u32[]{:S(2)}) copy-start(f32[2048,768]{1,0:T(8,128)} %get-tuple-element.284) | copy-start | bytes 18874372 | tf_op jit(solution)/shard_map/while
  109.6 5.0 %copy-start.1 = (f32[2048,768]{1,0:T(8,128)S(1)}, f32[2048,768]{1,0:T(8,128)}, u32[]{:S(2)}) copy-start(f32[2048,768]{1,0:T(8,128)} %get-tuple-element.284) | copy-start | bytes 18874372 | tf_op jit(solution)/shard_map/while
  120.8 4.9 %copy-start.1 = (f32[2048,768]{1,0:T(8,128)S(1)}, f32[2048,768]{1,0:T(8,128)}, u32[]{:S(2)}) copy-start(f32[2048,768]{1,0:T(8,128)} %get-tuple-element.284) | copy-start | bytes 18874372 | tf_op jit(solution)/shard_map/while
  131.9 4.9 %copy-start.1 = (f32[2048,768]{1,0:T(8,128)S(1)}, f32[2048,768]{1,0:T(8,128)}, u32[]{:S(2)}) copy-start(f32[2048,768]{1,0:T(8,128)} %get-tuple-element.284) | copy-start | bytes 18874372 | tf_op jit(solution)/shard_map/while
  143.0 4.9 %copy-start.1 = (f32[2048,768]{1,0:T(8,128)S(1)}, f32[2048,768]{1,0:T(8,128)}, u32[]{:S(2)}) copy-start(f32[2048,768]{1,0:T(8,128)} %get-tuple-element.284) | copy-start | bytes 18874372 | tf_op jit(solution)/shard_map/while
  149.3 61.0 %copy-start.2 = (bf16[1,48,3072]{2,1,0:T(8,128)(2,1)S(1)}, bf16[1,48,3072]{2,1,0:T(8,128)(2,1)}, u32[]{:S(2)}) copy-start(bf16[1,48,3072]{2,1,0:T(8,128)(2,1)} %param.12) | copy-start | bytes 884740
  150.2 22.3 %all-to-all-start.2 = ((bf16[32,24,1,128]{3,1,2,0:T(8,128)(2,1)}), bf16[32,24,1,128]{3,1,2,0:T(8,128)(2,1)S(1)}, u32[]{:S(2)}, u32[]{:S(2)}) async-start(bf16[32,24,1,128]{3,1,2,0:T(8,128)(2,1)} %bitcast.9), calls=%async_computation.2 | async-start | bytes 393216 | tf_op jit(solution)/shard_map/all_to_all | solution.py:113
  210.3 7.3 %copy-start.5 = (f32[1,48,64]{2,1,0:T(8,128)S(1)}, f32[1,48,64]{2,1,0:T(8,128)}, u32[]{:S(2)}) copy-start(f32[1,48,64]{2,1,0:T(8,128)} %param.17) | copy-start | bytes 36868
  210.3 11.7 %copy-start.4 = (f32[48,64]{1,0:T(8,128)S(1)}, f32[48,64]{1,0:T(8,128)}, u32[]{:S(2)}) copy-start(f32[48,64]{1,0:T(8,128)} %param.18) | copy-start | bytes 36868
  218.5 3.4 %collective-permute-start = (f32[48,64]{1,0:T(8,128)S(1)}, f32[48,64]{1,0:T(8,128)S(1)}, u32[]{:S(2)}, u32[]{:S(2)}) collective-permute-start(f32[48,64]{1,0:T(8,128)S(1)} %get-tuple-element.230), channel_id=1, source_target_pairs={{0,32},{32,64},{64,96},{96,128},{128,160},{160,192},{192,224},{1,3... | collective-permute-start | bytes 36872 | tf_op jit(solution)/shard_map/ppermute | solution.py:18
Sparse Core Ops, SparseCore 0:
  41.7 40.6 all-gather.2
  85.0 125.2 all-gather.4
where the time goes:
time: 232 us; the launch traced here: 229 us
  waiting for transfers between devices  82.7 us (36%)
  matrix products  69.3 us (30%)
  blocking collectives  32.1 us (14%)
  starting transfers between devices  16.6 us (7%)
  between operations  14.9 us (6%)
  other arithmetic  11.4 us (5%)
    all_gather x1, waiting for transfers between devices, body(): lax.all_gather(out_weight, 'seq', axis=0, tiled=True)  37.8 us
    all_to_all x1, blocking collectives, body(): lax.all_to_all(paired, 'seq', split_axis=1, concat_axis=2, tiled=True)  32.1 us
    dot_general x6, matrix products, fold_block(): jnp.einsum('hqk,khd->hqd', weights.astype(jnp.bfloat16), value_part, pref...  29.8 us
    dot_general x6, matrix products, fold_block(): jnp.einsum('qhd,khd->hqk', query_heads, key_part, preferred_element_type=...  28.2 us
    all_gather x1, waiting for transfers between devices, body(): lax.all_gather(own_pairs, 'queue', axis=1, tiled=True)  23.6 us
    all_to_all x1, starting transfers between devices, body(): lax.all_to_all(attended, 'seq', split_axis=0, concat_axis=2, tiled=True)  9.51 us
    all_to_all x1, waiting for transfers between devices, body(): lax.all_to_all(attended, 'seq', split_axis=0, concat_axis=2, tiled=True)  9.41 us
    all_to_all x1, waiting for transfers between devices, body(): lax.all_to_all(query_send, 'seq', split_axis=1, concat_axis=2, tiled=True)  9.11 us
  transfers between devices with their start and end apart: 5, of which 5 were waited for; matrix products, arithmetic and copies ran while one was open for 31% of the time, Pallas kernels for 0%

commit v1 on v0

v1 whole, which is shorter than its diff:
```python
import functools
import math

import jax
import jax.numpy as jnp
from jax import lax
from jax.experimental import pallas as pl
from jax.experimental.pallas import tpu as pltpu
from jax.sharding import PartitionSpec as P

D = 3072
H = 16
DH = 128
TEMB = 256
STRIDE = 125
NX, NC, NY, NZ = 4, 2, 4, 8
NQ = NX * NC
TOK = 48
COLS = D // NQ
LAT = 64
SCALE = DH**-0.5 * math.log2(math.e)
MESH = pl.DeviceIdType.MESH


def place(x, c, y, z):
    return {"queue": x * NC + c, "seq": z * NY + y}


def remote(src, dst, send_sem, recv_sem, device):
    return pltpu.make_async_remote_copy(
        src_ref=src,
        dst_ref=dst,
        send_sem=send_sem,
        recv_sem=recv_sem,
        device_id=device,
        device_id_type=MESH,
    )


def wait_bytes(ref, sem):
    pltpu.make_async_copy(ref, ref, sem).wait()


def attend(i, keys, values, q_buf, acc, peak):
    count = keys.shape[0]
    query = q_buf[:, i].reshape(NY * 2 * TOK, DH)
    extended = jnp.concatenate([values, jnp.ones_like(values)], axis=1)
    for part in range(3):
        rows = slice(part * 128, part * 128 + 128)
        scores = (
            lax.dot_general(
                query[rows], keys, (((1,), (1,)), ((), ())), preferred_element_type=jnp.float32
            )
            * SCALE
        )
        old = peak[i, rows, :]
        new = jnp.maximum(old, jnp.max(scores, axis=1, keepdims=True))
        factor = jnp.exp2(old - new)
        weights = jnp.exp2(scores - jnp.concatenate([new] * (count // 128), axis=1))
        mixed = jnp.dot(
            weights.astype(jnp.bfloat16), extended, preferred_element_type=jnp.float32
        )
        acc[i, rows, :] = acc[i, rows, :] * jnp.concatenate([factor, factor], axis=1) + mixed
        peak[i, rows, :] = new


def attend_pair(p, kv, q_buf, acc, peak):
    rows = NZ * TOK

    def both(i, carry):
        keys = kv[pl.ds(2 * p, 2), 0].reshape(2 * rows, DH)
        values = kv[pl.ds(2 * p, 2), 1].reshape(2 * rows, DH)
        attend(i, keys, values, q_buf, acc, peak)
        return carry

    lax.fori_loop(0, 2 * p + 1, both, 0)
    last = 2 * p + 1
    attend(
        last,
        kv[last, 0].reshape(rows, DH),
        kv[last, 1].reshape(rows, DH),
        q_buf,
        acc,
        peak,
    )


def mix_kernel(
    q_ref,
    k_ref,
    v_ref,
    hid_ref,
    act_ref,
    o_all,
    hid_all,
    act_all,
    kv,
    q_buf,
    acc,
    peak,
    o_part,
    o_recv,
    s_part,
    s_recv,
    merged,
    send_a,
    send_h,
    send_x,
    send_y,
    send_o,
    send_z,
    send_g,
    send_c,
    recv_kv,
    recv_q,
    recv_h,
    recv_x,
    recv_xr,
    recv_y,
    recv_yr,
    recv_o,
    recv_s,
    recv_z,
    recv_g,
    recv_gr,
    recv_c,
):
    queue = lax.axis_index("queue")
    seq = lax.axis_index("seq")
    x, c = queue // NC, queue % NC
    z, y = seq // NY, seq % NY
    xl, xr = (x + NX - 1) % NX, (x + 1) % NX
    yl, yr = (y + NY - 1) % NY, (y + 1) % NY
    y2 = (y + 2) % NY
    zk = z // 4
    xt = (z + queue) % NX

    def columns(ref, head):
        return ref.at[:, pl.ds(pl.multiple_of(head * DH, DH), DH)]

    def send_kv(j, carry):
        zt, ct = (z + j // 2) % NZ, (c + j % 2) % NC
        head = 2 * zt + ct
        device = place(x, ct, y, zt)
        remote(
            columns(k_ref, head), kv.at[queue, 0, z], send_a.at[0], recv_kv.at[c], device
        ).start()
        remote(
            columns(v_ref, head), kv.at[queue, 1, z], send_a.at[0], recv_kv.at[c], device
        ).start()
        return carry

    lax.fori_loop(1, 16, send_kv, 0)
    own_head = 2 * z + c
    pltpu.make_async_copy(columns(k_ref, own_head), kv.at[queue, 0, z], recv_kv.at[c]).start()
    pltpu.make_async_copy(columns(v_ref, own_head), kv.at[queue, 1, z], recv_kv.at[c]).start()

    def send_q(j, carry):
        zt, ct = (z + j // 2) % NZ, (c + j % 2) % NC
        remote(
            columns(q_ref, 2 * zt + ct),
            q_buf.at[y, queue, zk],
            send_a.at[1],
            recv_q.at[0],
            place(xt, ct, y, zt),
        ).start()
        return carry

    lax.fori_loop(1, 16, send_q, 0)

    @pl.when(xt != x)
    def _():
        remote(
            columns(q_ref, own_head),
            q_buf.at[y, queue, zk],
            send_a.at[2],
            recv_q.at[0],
            place(xt, c, y, z),
        ).start()

    @pl.when(xt == x)
    def _():
        pltpu.make_async_copy(
            columns(q_ref, own_head), q_buf.at[y, queue, zk], recv_q.at[0]
        ).start()

    def hidden_part(d):
        to = (queue + d) % NQ
        return remote(
            hid_ref.at[:, pl.ds(pl.multiple_of(to * COLS, 128), COLS)],
            hid_all.at[queue],
            send_h.at[0],
            recv_h.at[0],
            {"queue": to, "seq": seq},
        )

    def act_part(d):
        to = (queue + d) % NQ
        return remote(
            act_ref,
            act_all.at[queue],
            send_h.at[1],
            recv_h.at[1],
            {"queue": to, "seq": seq},
        )

    def send_hidden(d, carry):
        hidden_part(d).start()
        act_part(d).start()
        return carry

    lax.fori_loop(1, NQ, send_hidden, 0)
    pltpu.make_async_copy(
        hid_ref.at[:, pl.ds(pl.multiple_of(queue * COLS, 128), COLS)],
        hid_all.at[queue],
        recv_h.at[0],
    ).start()
    pltpu.make_async_copy(act_ref, act_all.at[queue], recv_h.at[1]).start()

    acc[...] = jnp.zeros_like(acc)
    peak[...] = jnp.full_like(peak, -1e30)

    for blk in range(2):
        mine = 2 * x + blk
        wait_bytes(kv.at[mine], recv_kv.at[blk])
        for side, to in ((0, xr), (1, xl)):
            remote(
                kv.at[mine],
                kv.at[mine],
                send_x.at[blk, side],
                recv_x.at[blk, side],
                place(to, c, y, z),
            ).start()

    wait_bytes(q_buf.at[y], recv_q.at[0])
    for side, to in ((0, yr), (1, yl)):
        remote(
            q_buf.at[y], q_buf.at[y], send_y.at[side], recv_y.at[side], place(x, c, to, z)
        ).start()
    wait_bytes(q_buf.at[yl], recv_y.at[0])
    remote(
        q_buf.at[yl, pl.ds(0, 4)],
        q_buf.at[yl, pl.ds(0, 4)],
        send_y.at[2],
        recv_yr.at[0],
        place(x, c, yr, z),
    ).start()
    wait_bytes(q_buf.at[yr], recv_y.at[1])
    remote(
        q_buf.at[yr, pl.ds(4, 4)],
        q_buf.at[yr, pl.ds(4, 4)],
        send_y.at[3],
        recv_yr.at[1],
        place(x, c, yl, z),
    ).start()
    wait_bytes(q_buf.at[y2, pl.ds(0, 4)], recv_yr.at[0])
    wait_bytes(q_buf.at[y2, pl.ds(4, 4)], recv_yr.at[1])

    attend_pair(x, kv, q_buf, acc, peak)

    wait_bytes(kv.at[2 * xl], recv_x.at[0, 0])
    remote(
        kv.at[2 * xl], kv.at[2 * xl], send_x.at[0, 2], recv_xr.at[0], place(xr, c, y, z)
    ).start()
    wait_bytes(kv.at[2 * xl + 1], recv_x.at[1, 0])
    wait_bytes(kv.at[2 * xr + 1], recv_x.at[1, 1])
    remote(
        kv.at[2 * xr + 1], kv.at[2 * xr + 1], send_x.at[1, 2], recv_xr.at[1], place(xl, c, y, z)
    ).start()
    attend_pair(xl, kv, q_buf, acc, peak)
    wait_bytes(kv.at[2 * xr], recv_x.at[0, 1])
    attend_pair(xr, kv, q_buf, acc, peak)
    x2 = (x + 2) % NX
    wait_bytes(kv.at[2 * x2], recv_xr.at[0])
    wait_bytes(kv.at[2 * x2 + 1], recv_xr.at[1])
    attend_pair(x2, kv, q_buf, acc, peak)

    lane = lax.broadcasted_iota(jnp.int32, (2 * TOK, 128), 1)
    row = lax.broadcasted_iota(jnp.int32, (2 * TOK, 128), 0)
    diagonal = lane == row

    def finish(g, carry):
        total = acc[g, :, 128:]
        out = (acc[g, :, :128] / total).astype(jnp.bfloat16)
        level = peak[g] + jnp.log2(total)
        for part in range(NY):
            rows = slice(part * 2 * TOK, (part + 1) * 2 * TOK)
            o_part[part, g] = out[rows].reshape(2, TOK, DH)
            s_part[part, pl.ds(g, 1), :] = jnp.sum(
                jnp.where(diagonal, level[rows], 0.0), axis=0, keepdims=True
            )
        return carry

    lax.fori_loop(0, NQ, finish, 0)

    def partial_copies(d):
        to = (y + d) % NY
        device = place(x, c, to, z)
        return (
            remote(o_part.at[to], o_recv.at[y], send_o.at[d - 1, 0], recv_o.at[d - 1], device),
            remote(s_part.at[to], s_recv.at[y], send_o.at[d - 1, 1], recv_s.at[d - 1], device),
        )

    for d in (2, 1, 3):
        for copy in partial_copies(d):
            copy.start()
    for d in (1, 2, 3):
        source = (y + NY - d) % NY
        wait_bytes(o_recv.at[source], recv_o.at[d - 1])
        wait_bytes(s_recv.at[source], recv_s.at[d - 1])

    def column(vector):
        return jnp.sum(
            jnp.where(diagonal, jnp.broadcast_to(vector, (2 * TOK, 128)), 0.0),
            axis=1,
            keepdims=True,
        )

    def merge(g, carry):
        levels = [column(s_part[y, pl.ds(g, 1), :])]
        outs = [o_part[y, g]]
        for d in (1, 2, 3):
            source = (y + d) % NY
            levels.append(column(s_recv[source, pl.ds(g, 1), :]))
            outs.append(o_recv[source, g])
        top = functools.reduce(jnp.maximum, levels)
        shares = [jnp.exp2(level - top) for level in levels]
        total = functools.reduce(jnp.add, shares)
        mixed = functools.reduce(
            jnp.add,
            [
                share * out.reshape(2 * TOK, DH).astype(jnp.float32)
                for share, out in zip(shares, outs)
            ],
        )
        merged[g] = (mixed / total).astype(jnp.bfloat16).reshape(2, TOK, DH)
        for half in range(2):
            zt = (x + 8 - g) % 4 + 4 * half

            @pl.when(zt != z)
            def _():
                remote(
                    merged.at[g, half],
                    o_all.at[c, g, z],
                    send_z.at[0],
                    recv_z.at[0],
                    place(x, c, y, zt),
                ).start()

            @pl.when(zt == z)
            def _():
                pltpu.make_async_copy(
                    merged.at[g, half], o_all.at[c, g, z], recv_z.at[0]
                ).start()

        return carry

    lax.fori_loop(0, NQ, merge, 0)

    other = place(x, 1 - c, y, z)

    def across(g, slot):
        return remote(o_all.at[c, g], o_all.at[c, g], send_c.at[slot], recv_c.at[slot], other)

    def firsts(xs):
        return (xs + 8 - z) % 4

    mine = firsts(x)
    wait_bytes(o_all.at[c, pl.ds(0, 2)], recv_z.at[0])
    for half in range(2):
        g = mine + 4 * half
        for side, to in ((0, xr), (1, xl)):
            remote(
                o_all.at[c, g],
                o_all.at[c, g],
                send_g.at[half, side],
                recv_g.at[half, side],
                place(to, c, y, z),
            ).start()
    across(mine, 0).start()
    across(mine + 4, 1).start()
    left, right, far = firsts(xl), firsts(xr), firsts(x2)
    wait_bytes(o_all.at[c, left], recv_g.at[0, 0])
    remote(
        o_all.at[c, left], o_all.at[c, left], send_g.at[0, 2], recv_gr.at[0], place(xr, c, y, z)
    ).start()
    across(left, 2).start()
    wait_bytes(o_all.at[c, right + 4], recv_g.at[1, 1])
    remote(
        o_all.at[c, right + 4],
        o_all.at[c, right + 4],
        send_g.at[1, 2],
        recv_gr.at[1],
        place(xl, c, y, z),
    ).start()
    across(right + 4, 3).start()
    wait_bytes(o_all.at[c, left + 4], recv_g.at[1, 0])
    across(left + 4, 4).start()
    wait_bytes(o_all.at[c, right], recv_g.at[0, 1])
    across(right, 5).start()
    wait_bytes(o_all.at[c, far], recv_gr.at[0])
    across(far, 6).start()
    wait_bytes(o_all.at[c, far + 4], recv_gr.at[1])
    across(far + 4, 7).start()

    wait_bytes(hid_all, recv_h.at[0])
    wait_bytes(act_all, recv_h.at[1])
    wait_bytes(hid_all.at[pl.ds(0, 7)], send_h.at[0])
    wait_bytes(act_all.at[pl.ds(0, 7)], send_h.at[1])
    wait_bytes(q_buf.at[pl.ds(0, 3), pl.ds(0, 5)], send_a.at[0])
    wait_bytes(q_buf.at[pl.ds(0, 3), pl.ds(0, 5), 0], send_a.at[1])

    @pl.when(xt != x)
    def _():
        wait_bytes(q_buf.at[0, 0, 0], send_a.at[2])

    for blk in range(2):
        for side in range(3):
            wait_bytes(kv.at[0], send_x.at[blk, side])
            wait_bytes(o_all.at[0, 0], send_g.at[blk, side])
    wait_bytes(q_buf.at[0], send_y.at[0])
    wait_bytes(q_buf.at[0], send_y.at[1])
    wait_bytes(q_buf.at[0, pl.ds(0, 4)], send_y.at[2])
    wait_bytes(q_buf.at[0, pl.ds(0, 4)], send_y.at[3])
    for d in (1, 2, 3):
        for copy in partial_copies(d):
            copy.wait_send()

    wait_bytes(merged.at[pl.ds(0, 7)], send_z.at[0])
    for slot in range(8):
        copy = across(slot, slot)
        copy.wait_send()
        copy.wait_recv()


def mix(queries, keys, values, hidden, activated):
    bf16, f32 = jnp.bfloat16, jnp.float32
    dma = pltpu.SemaphoreType.DMA
    any_spec = pl.BlockSpec(memory_space=pl.ANY)
    return pl.pallas_call(
        mix_kernel,
        out_shape=(
            jax.ShapeDtypeStruct((NC, NQ, NZ, TOK, DH), bf16),
            jax.ShapeDtypeStruct((NQ, TOK, COLS), bf16),
            jax.ShapeDtypeStruct((NQ, 8, TEMB), f32),
        ),
        in_specs=[any_spec] * 5,
        out_specs=(any_spec,) * 3,
        scratch_shapes=[
            pltpu.VMEM((NQ, 2, NZ, TOK, DH), bf16),
            pltpu.VMEM((NY, NQ, 2, TOK, DH), bf16),
            pltpu.VMEM((NQ, NY * 2 * TOK, 256), f32),
            pltpu.VMEM((NQ, NY * 2 * TOK, 128), f32),
            pltpu.VMEM((NY, NQ, 2, TOK, DH), bf16),
            pltpu.VMEM((NY, NQ, 2, TOK, DH), bf16),
            pltpu.VMEM((NY, NQ, 128), f32),
            pltpu.VMEM((NY, NQ, 128), f32),
            pltpu.VMEM((NQ, 2, TOK, DH), bf16),
            dma((3,)),
            dma((2,)),
            dma((2, 3)),
            dma((4,)),
            dma((3, 2)),
            dma((1,)),
            dma((2, 3)),
            dma((8,)),
            dma((2,)),
            dma((1,)),
            dma((2,)),
            dma((2, 2)),
            dma((2,)),
            dma((2,)),
            dma((2,)),
            dma((3,)),
            dma((3,)),
            dma((1,)),
            dma((2, 2)),
            dma((2,)),
            dma((8,)),
        ],
        compiler_params=pltpu.CompilerParams(
            has_side_effects=True, vmem_limit_bytes=40 * 1024 * 1024
        ),
        cost_estimate=pl.CostEstimate(
            flops=3_000_000_000, bytes_accessed=8_000_000, transcendentals=6_000_000
        ),
        name="mix",
    )(queries, keys, values, hidden, activated)


def project_kernel(
    o_ref,
    w_ref,
    hid_ref,
    act_ref,
    mod_ref,
    final_ref,
    lat_ref,
    fresh_ref,
    vel_ref,
    next_ref,
    mod_buf,
    final_buf,
    message,
    received,
    update,
    arrived,
    load_sem,
    send_sem,
    recv_sem,
    move_sem,
):
    queue = lax.axis_index("queue")
    seq = lax.axis_index("seq")
    barrier = pltpu.get_barrier_semaphore()

    def greet(d, carry):
        pl.semaphore_signal(
            barrier,
            inc=1,
            device_id={"queue": (queue + d) % NQ, "seq": seq},
            device_id_type=MESH,
        )
        return carry

    lax.fori_loop(1, NQ, greet, 0)
    loads = [
        pltpu.make_async_copy(
            mod_ref.at[:, pl.ds(pl.multiple_of(part * D + queue * COLS, 128), COLS)],
            mod_buf.at[part],
            load_sem.at[part],
        )
        for part in range(3)
    ]
    loads.append(
        pltpu.make_async_copy(
            final_ref.at[pl.ds(pl.multiple_of(queue * COLS, 128), COLS), :],
            final_buf,
            load_sem.at[3],
        )
    )
    for load in loads:
        load.start()

    projected = None
    for parity in range(NC):
        for zh in range(0, NZ, 2):
            left = jnp.concatenate(
                [o_ref[parity, :, zh + k].reshape(NQ * TOK, DH) for k in range(2)], axis=1
            )
            heads = [2 * (zh + k) + parity for k in range(2)]
            right = jnp.concatenate([w_ref[h * DH : (h + 1) * DH, :] for h in heads], axis=0)
            term = jnp.dot(left, right, preferred_element_type=jnp.float32)
            projected = term if projected is None else projected + term

    for load in loads:
        load.wait()
    act = act_ref[:, 0, :].astype(jnp.bfloat16)
    gate, shift, scale = (
        jnp.dot(act, mod_buf[part], preferred_element_type=jnp.float32) for part in range(3)
    )
    scale = 1.0 + scale
    final = final_buf[...]
    final32 = final.astype(jnp.float32)
    scale_sum = jnp.dot(
        scale, final32, preferred_element_type=jnp.float32, precision=lax.Precision.HIGHEST
    )
    shift_sum = jnp.dot(
        shift, final32, preferred_element_type=jnp.float32, precision=lax.Precision.HIGHEST
    )
    lane = lax.broadcasted_iota(jnp.int32, (TOK, LAT), 1)
    for g in range(NQ):
        rows = slice(g * TOK, (g + 1) * TOK)
        stream = hid_ref[g].astype(jnp.float32) + gate[g : g + 1] * projected[rows]
        center = jnp.mean(stream, axis=1, keepdims=True)
        apart = stream - center
        spread = jnp.sum(apart * apart, axis=1, keepdims=True)
        scaled = (apart * scale[g : g + 1]).astype(jnp.bfloat16)
        message[g, 0:TOK, 0:LAT] = jnp.dot(scaled, final, preferred_element_type=jnp.float32)
        message[g, 0:TOK, LAT:] = jnp.where(
            lane == 0, center, jnp.where(lane == 1, spread, 0.0)
        )
        message[g, TOK : TOK + 8, 0:LAT] = jnp.broadcast_to(scale_sum[g : g + 1], (8, LAT))
        message[g, TOK : TOK + 8, LAT:] = jnp.broadcast_to(shift_sum[g : g + 1], (8, LAT))

    def part(d):
        to = (queue + d) % NQ
        return remote(
            message.at[to],
            received.at[queue],
            send_sem.at[d - 1],
            recv_sem.at[d - 1],
            {"queue": to, "seq": seq},
        )

    pl.semaphore_wait(barrier, NQ - 1)
    for d in range(1, NQ):
        part(d).start()
    blocks = [message[queue]]
    for d in range(1, NQ):
        part(d).wait_recv()
        blocks.append(received[(queue + NQ - d) % NQ])
    centers = [block[0:TOK, LAT : LAT + 1] for block in blocks]
    center = functools.reduce(jnp.add, centers) / NQ
    summed = functools.reduce(jnp.add, [block[0:TOK, LAT + 1 : LAT + 2] for block in blocks])
    mixed = functools.reduce(jnp.add, [block[0:TOK, 0:LAT] for block in blocks])
    offset = functools.reduce(jnp.add, [block[TOK : TOK + 1, LAT:] for block in blocks])
    for block, local in zip(blocks, centers):
        away = local - center
        summed = summed + COLS * (away * away)
        mixed = mixed + away * block[TOK : TOK + 1, 0:LAT]
    velocity = mixed / jnp.sqrt(summed / D + 1e-06) + offset
    vel_ref[...] = velocity
    update[:, 0:LAT] = lat_ref[...] - STRIDE / 1000.0 * velocity
    update[:, LAT:] = jnp.zeros((TOK, LAT), jnp.float32)
    behind = remote(
        update,
        arrived,
        move_sem.at[0],
        move_sem.at[1],
        {"queue": (queue + 1) % NQ, "seq": seq},
    )

    behind.start()
    behind.wait_recv()
    next_ref[...] = jnp.where(queue == 0, fresh_ref[...], arrived[:, 0:LAT])
    behind.wait_send()
    for d in range(1, NQ):
        part(d).wait_send()


def project(o_all, weight, hid_all, act_all, mod_weight, final_weight, latents, fresh):
    f32, bf16 = jnp.float32, jnp.bfloat16
    dma = pltpu.SemaphoreType.DMA
    vmem = pl.BlockSpec(memory_space=pltpu.VMEM)
    any_spec = pl.BlockSpec(memory_space=pl.ANY)
    return pl.pallas_call(
        project_kernel,
        out_shape=(jax.ShapeDtypeStruct((TOK, LAT), f32),) * 2,
        in_specs=[vmem] * 4 + [any_spec] * 2 + [vmem] * 2,
        out_specs=(vmem, vmem),
        scratch_shapes=[
            pltpu.VMEM((3, TEMB, COLS), bf16),
            pltpu.VMEM((COLS, LAT), bf16),
            pltpu.VMEM((NQ, TOK + 8, 128), f32),
            pltpu.VMEM((NQ, TOK + 8, 128), f32),
            pltpu.VMEM((TOK, 128), f32),
            pltpu.VMEM((TOK, 128), f32),
            dma((4,)),
            dma((NQ - 1,)),
            dma((NQ - 1,)),
            dma((2,)),
        ],
        compiler_params=pltpu.CompilerParams(
            collective_id=1, has_side_effects=True, vmem_limit_bytes=40 * 1024 * 1024
        ),
        name="project",
    )(o_all, weight, hid_all, act_all, mod_weight, final_weight, latents, fresh)


def time_embed(step_values):
    halfway = TEMB // 2
    freqs = jnp.exp(-math.log(10000.0) * jnp.arange(halfway, dtype=jnp.float32) / halfway)
    angles = step_values.astype(jnp.float32)[:, None] * freqs[None, :]
    return jnp.concatenate([jnp.cos(angles), jnp.sin(angles)], axis=1)


def body(
    hidden,
    queries,
    keys,
    values,
    timesteps,
    latents,
    fresh_noise,
    out_weight,
    mod_weight,
    final_weight,
):
    queue = lax.axis_index("queue")
    own_columns = lax.dynamic_slice_in_dim(out_weight, queue * COLS, COLS, 1)
    weight = lax.all_gather(own_columns, "seq", axis=0, tiled=True)
    activated = jax.nn.silu(time_embed(timesteps)).astype(jnp.bfloat16).astype(jnp.float32)
    activated = jnp.broadcast_to(activated, (8, TEMB))
    o_all, hid_all, act_all = mix(queries[0], keys[0], values[0], hidden[0], activated)
    velocity, following = project(
        o_all, weight, hid_all, act_all, mod_weight, final_weight, latents[0], fresh_noise
    )
    return velocity[None], following[None]


def solution(mesh):
    placed = (
        P("queue", "seq", None),
        P("queue", "seq", None),
        P("queue", "seq", None),
        P("queue", "seq", None),
        P("queue"),
        P("queue", "seq", None),
        P("seq", None),
        P("seq", None),
        P(),
        P(),
    )
    return jax.shard_map(
        body,
        mesh=mesh,
        in_specs=placed,
        out_specs=(P("queue", "seq", None), P("queue", "seq", None)),
        check_vma=False,
    )
```

time: 232 us -> 129 us (0.56)
  Pallas kernels: 0 us -> 100 us
  waiting for transfers between devices: 82.7 us -> 0.04 us
  matrix products: 69.3 us -> 0 us
  blocking collectives: 32.1 us -> 0 us
  starting transfers between devices: 16.6 us -> 0.04 us
  other arithmetic: 11.4 us -> 0.07 us
  local copies, waits for them, and re-layouts: 1.97 us -> 11.6 us
    pallas_call x0 -> x2, Pallas kernels: none -> 100 us  [the longest x1 92.2 us: mix(): pl.pallas_call(mix_kernel, out_shape=(jax.ShapeDtypeStruct((NC, NQ, NZ, T...]
    dot_general x15 -> x0, matrix products: 69.3 us -> none  [the longest x6 29.8 us: fold_block(): jnp.einsum('hqk,khd->hqd', weights.astype(jnp.bfloat16), value_part, pref...]
    all_gather x2 -> x1, waiting for transfers between devices: 61.4 us -> 0.02 us  [body(): weight = lax.all_gather(own_columns, 'seq', axis=0, tiled=True)]
    all_to_all x1 -> x0, blocking collectives: 32.1 us -> none  [body(): lax.all_to_all(paired, 'seq', split_axis=1, concat_axis=2, tiled=True)]
    all_to_all x2 -> x0, waiting for transfers between devices: 18.5 us -> none  [the longest x1 9.41 us: body(): lax.all_to_all(attended, 'seq', split_axis=0, concat_axis=2, tiled=True)]
    all_to_all x2 -> x0, starting transfers between devices: 15.3 us -> none  [the longest x1 9.51 us: body(): lax.all_to_all(attended, 'seq', split_axis=0, concat_axis=2, tiled=True)]
    unnamed x11 -> x21, local copies, waits for them, and re-layouts: 0.06 us -> 11 us
    reduce_sum x7 -> x0, other arithmetic: 8.26 us -> none  [the longest x6 8.02 us: fold_block(): new_total = running_total * factor + jnp.sum(weights, axis=2)]
  transfers between devices with their start and end apart: 5 -> 1, of which waited for: 5 -> 0; matrix products, arithmetic and copies ran while one was open for 31% -> 1% of each run, Pallas kernels for 0% -> 73%
where the time goes in v1:
time: 129 us; the launch traced here: 127 us
  Pallas kernels  100 us (78%)
  between operations  14.8 us (11%)
  local copies, waits for them, and re-layouts  11.6 us (9%)
    pallas_call x1, Pallas kernels, mix(): pl.pallas_call(mix_kernel, out_shape=(jax.ShapeDtypeStruct((NC, NQ, NZ, T...  92.2 us
    unnamed x21, local copies, waits for them, and re-layouts  11 us
    pallas_call x1, Pallas kernels, project(): pl.pallas_call(project_kernel, out_shape=(jax.ShapeDtypeStruct((TOK, LAT)...  8.04 us
  transfers between devices with their start and end apart: 1, of which 0 were waited for; matrix products, arithmetic and copies ran while one was open for 1% of the time, Pallas kernels for 73%

profile of v1, /device:TPU:7, one launch (start us, length us, event | category | flops | bytes accessed | tf_op | source)
XLA Modules:
  0.0 126.8 jit_solution(8436194964899271748)
XLA Ops:
  7.2 0.0 copy-start
  7.2 0.0 all-gather.2.cloned.1.call-start
  7.2 0.9 copy-done
  8.2 0.6 constant_dynamic-slice_fusion
  8.8 0.0 all-gather.2.cloned.1.call-update
  9.5 1.4 %copy.12.final_ref = bf16[3072,64]{1,0:T(8,128)(2,1)S(1)} copy(bf16[3072,64]{0,1:T(8,128)(2,1)} %param.19) | data formatting | bytes 786432 | tf_op args[9]
  10.8 0.1 fusion.2
  10.9 0.0 copy-start.5
  10.9 1.0 copy-done.5
  11.9 0.0 copy-start.6
  11.9 0.9 copy-done.6
  12.8 0.0 copy-start.7
  12.8 0.9 copy-done.7
  13.7 0.0 copy-start.8
  13.7 0.9 copy-done.8
  14.7 0.0 copy-start.3
  14.7 0.0 copy-start.4
  14.7 92.2 %mix.1 = (bf16[2,8,8,48,128]{4,3,2,1,0:T(8,128)(2,1)S(1)}, bf16[8,48,384]{2,1,0:T(8,128)(2,1)S(1)}, f32[8,8,256]{2,1,0:T(8,128)S(1)}) custom-call(bf16[48,2048]{1,0:T(8,128)(2,1)S(1)} %bitcast.12, bf16[48,2048]{1,0:T(8,128)(2,1)S(1)} %bitcast.13, bf16[48,2048]{1,0:T(8,128)(2,1)S(1)} %bitcast.14, bf16[48,3072]{1,0:T(8,128)(2,1)S(1)} %bitcast.11, ...), custom_call_target="tpu_custom_call" | custom-call | flops 3000000000 | bytes 8000000 | tf_op jit(solution)/shard_map/mix/pallas_call | solution.py:440
  106.9 0.0 all-gather.2.cloned.1.call-done.w_ref
  106.9 0.0 copy-done.3
  106.9 0.0 copy-done.4
  106.9 0.0 copy-start.1
  106.9 2.3 %copy-done.1 = bf16[256,9216]{1,0:T(8,128)(2,1)S(1)} copy-done((bf16[256,9216]{1,0:T(8,128)(2,1)S(1)}, bf16[256,9216]{1,0:T(8,128)(2,1)}, u32[]{:S(2)}) %copy-start.1) | copy-done | bytes 4718616
  109.3 0.0 copy-start.2
  109.3 1.4 %copy-done.2 = bf16[2048,384]{1,0:T(8,128)(2,1)S(1)} copy-done((bf16[2048,384]{1,0:T(8,128)(2,1)S(1)}, bf16[2048,384]{1,0:T(8,128)(2,1)}, u32[]{:S(2)}) %copy-start.2) | copy-done | bytes 1572888
  110.7 8.0 %project.1 = (f32[48,64]{1,0:T(8,128)S(1)}, f32[48,64]{1,0:T(8,128)S(1)}) custom-call(bf16[2,8,8,48,128]{4,3,2,1,0:T(8,128)(2,1)S(1)} %get-tuple-element.7.o_ref, bf16[2048,384]{1,0:T(8,128)(2,1)S(1)} %copy-done.2, bf16[8,48,384]{2,1,0:T(8,128)(2,1)S(1)} %get-tuple-element.8.hid_ref, f32[8,8,256]{2,1,0:T(8,128)S(1)} %get-tuple-element.9.act_ref, ...), custom_call_target="tpu_custom_call" | custom-call | tf_op jit(solution)/shard_map/project/pallas_call | solution.py:637
  118.7 0.6 copy.16
  119.3 0.6 copy.17
  (2 shorter events, 0.0 us)
Async XLA Ops:
  7.2 1.0 copy-start
  7.2 99.7 %all-gather.2.cloned.1.call-start = ((), (), s32[]{:S(2)}) async-start(), calls=%async_computation | async-start | bytes 1622016 | tf_op jit(solution)/shard_map/all_gather | solution.py:682
  10.9 1.0 copy-start.5
  11.9 0.9 copy-start.6
  12.8 0.9 copy-start.7
  13.7 0.9 copy-start.8
  14.7 92.2 %copy-start.3 = (f32[1,48,64]{2,1,0:T(8,128)S(1)}, f32[1,48,64]{2,1,0:T(8,128)}, u32[]{:S(2)}) copy-start(f32[1,48,64]{2,1,0:T(8,128)} %param.15) | copy-start | bytes 36868
  14.7 92.3 %copy-start.4 = (f32[48,64]{1,0:T(8,128)S(1)}, f32[48,64]{1,0:T(8,128)}, u32[]{:S(2)}) copy-start(f32[48,64]{1,0:T(8,128)} %fresh_ref.1) | copy-start | bytes 36868
  106.9 2.3 %copy-start.1 = (bf16[256,9216]{1,0:T(8,128)(2,1)S(1)}, bf16[256,9216]{1,0:T(8,128)(2,1)}, u32[]{:S(2)}) copy-start(bf16[256,9216]{1,0:T(8,128)(2,1)} %mod_ref.1) | copy-start | bytes 14155780
  109.3 1.4 %copy-start.2 = (bf16[2048,384]{1,0:T(8,128)(2,1)S(1)}, bf16[2048,384]{1,0:T(8,128)(2,1)}, u32[]{:S(2)}) copy-start(bf16[2048,384]{1,0:T(8,128)(2,1)} %all-gather.2.cloned.1.call-done.w_ref) | copy-start | bytes 4718596
Sparse Core Ops, SparseCore 0:
  10.6 82.8 all-gather.1

commit v2 on v0

v2 whole, which is shorter than its diff:
```python
import functools
import math

import jax
import jax.numpy as jnp
from jax import lax
from jax.experimental import pallas as pl
from jax.experimental.pallas import tpu as pltpu
from jax.sharding import PartitionSpec as P

D = 3072
H = 16
DH = 128
TEMB = 256
STRIDE = 125
NX, NC, NY, NZ = 4, 2, 4, 8
NQ = NX * NC
TOK = 48
COLS = D // NQ
LAT = 64
ROWS = 2 * TOK
PART = ROWS + 16
SCALE = DH**-0.5 * math.log2(math.e)
MESH = pl.DeviceIdType.MESH


def place(x, c, y, z):
    return {"queue": x * NC + c, "seq": z * NY + y}


def remote(src, dst, send_sem, recv_sem, device):
    return pltpu.make_async_remote_copy(
        src_ref=src,
        dst_ref=dst,
        send_sem=send_sem,
        recv_sem=recv_sem,
        device_id=device,
        device_id_type=MESH,
    )


def wait_bytes(ref, sem):
    pltpu.make_async_copy(ref, ref, sem).wait()


def attend(i, keys, values, q_buf, acc, peak):
    count = keys.shape[0]
    query = q_buf[:, i].reshape(NY * 2 * TOK, DH)
    extended = jnp.concatenate([values, jnp.ones_like(values)], axis=1)
    for part in range(3):
        rows = slice(part * 128, part * 128 + 128)
        scores = (
            lax.dot_general(
                query[rows], keys, (((1,), (1,)), ((), ())), preferred_element_type=jnp.float32
            )
            * SCALE
        )
        old = peak[i, rows, :]
        new = jnp.maximum(old, jnp.max(scores, axis=1, keepdims=True))
        factor = jnp.exp2(old - new)
        weights = jnp.exp2(scores - jnp.concatenate([new] * (count // 128), axis=1))
        mixed = jnp.dot(
            weights.astype(jnp.bfloat16), extended, preferred_element_type=jnp.float32
        )
        acc[i, rows, :] = acc[i, rows, :] * jnp.concatenate([factor, factor], axis=1) + mixed
        peak[i, rows, :] = new


def fused_kernel(
    q_ref,
    k_ref,
    v_ref,
    hid_ref,
    w_ref,
    step_ref,
    mod_ref,
    final_ref,
    lat_ref,
    fresh_ref,
    out_ref,
    kv,
    q_buf,
    acc,
    peak,
    o_part,
    o_recv,
    merged,
    o_all,
    hid_all,
    act_all,
    w_all,
    mod_buf,
    final_buf,
    lat_buf,
    fresh_buf,
    consts,
    sums,
    message,
    received,
    update,
    arrived,
    load_sem,
    send_a,
    send_h,
    send_w_ref,
    send_x,
    send_y,
    send_o,
    send_z,
    send_g,
    send_c,
    send_m,
    recv_kv,
    recv_q,
    recv_h,
    recv_wz,
    recv_wy,
    recv_x,
    recv_xr,
    recv_y,
    recv_o,
    recv_z,
    recv_g,
    recv_c,
    recv_m,
    move_sem,
):
    queue = lax.axis_index("queue")
    seq = lax.axis_index("seq")
    x, c = queue // NC, queue % NC
    z, y = seq // NY, seq % NY
    xl, xr = (x + NX - 1) % NX, (x + 1) % NX
    zk = z // 4
    xt = (z + queue) % NX
    own_head = 2 * z + c
    barrier = pltpu.get_barrier_semaphore()

    def greet(j, carry):
        device = place((x + j // 16) % NX, (c + j % 2) % NC, y, (z + (j // 2) % 8) % NZ)
        pl.semaphore_signal(barrier, inc=1, device_id=device, device_id_type=MESH)
        return carry

    lax.fori_loop(1, 64, greet, 0)
    for d in (1, 2, 3):
        pl.semaphore_signal(
            barrier, inc=1, device_id=place(x, c, (y + d) % NY, z), device_id_type=MESH
        )

    def own_columns(part):
        return pl.ds(pl.multiple_of(part * D + queue * COLS, 128), COLS)

    loads = [
        pltpu.make_async_copy(mod_ref.at[:, own_columns(n)], mod_buf.at[n], load_sem.at[n])
        for n in range(3)
    ]
    loads.append(pltpu.make_async_copy(final_ref.at[:, own_columns(0)], final_buf, load_sem.at[3]))
    loads.append(pltpu.make_async_copy(lat_ref, lat_buf, load_sem.at[4]))
    loads.append(pltpu.make_async_copy(fresh_ref, fresh_buf, load_sem.at[5]))
    for load in loads:
        load.start()

    halfway = TEMB // 2
    index = lax.broadcasted_iota(jnp.int32, (8, halfway), 1).astype(jnp.float32)
    angles = step_ref[0].astype(jnp.float32) * jnp.exp(-math.log(10000.0) * index / halfway)
    embed = jnp.concatenate([jnp.cos(angles), jnp.sin(angles)], axis=1)
    act_all[queue] = embed / (1.0 + jnp.exp(-embed))
    acc[...] = jnp.zeros_like(acc)
    peak[...] = jnp.full_like(peak, -1e30)
    pl.semaphore_wait(barrier, 66)

    def columns(ref, head):
        return ref.at[:, pl.ds(pl.multiple_of(head * DH, DH), DH)]

    def send_q(j, carry):
        zt, ct = (z + j // 2) % NZ, (c + j % 2) % NC
        remote(
            columns(q_ref, 2 * zt + ct),
            q_buf.at[y, queue, zk],
            send_a.at[1],
            recv_q.at[0],
            place(xt, ct, y, zt),
        ).start()
        return carry

    lax.fori_loop(1, 16, send_q, 0)

    @pl.when(xt != x)
    def _():
        remote(
            columns(q_ref, own_head),
            q_buf.at[y, queue, zk],
            send_a.at[2],
            recv_q.at[0],
            place(xt, c, y, z),
        ).start()

    @pl.when(xt == x)
    def _():
        pltpu.make_async_copy(
            columns(q_ref, own_head), q_buf.at[y, queue, zk], recv_q.at[0]
        ).start()

    def send_kv(j, carry):
        zt, ct = (z + j // 2) % NZ, (c + j % 2) % NC
        head = 2 * zt + ct
        device = place(x, ct, y, zt)
        remote(
            columns(k_ref, head), kv.at[queue, 0, z], send_a.at[0], recv_kv.at[c], device
        ).start()
        remote(
            columns(v_ref, head), kv.at[queue, 1, z], send_a.at[0], recv_kv.at[c], device
        ).start()
        return carry

    lax.fori_loop(1, 16, send_kv, 0)
    pltpu.make_async_copy(columns(k_ref, own_head), kv.at[queue, 0, z], recv_kv.at[c]).start()
    pltpu.make_async_copy(columns(v_ref, own_head), kv.at[queue, 1, z], recv_kv.at[c]).start()

    def send_hidden(d, carry):
        to = (queue + d) % NQ
        device = {"queue": to, "seq": seq}
        remote(
            act_all.at[queue], act_all.at[queue], send_h.at[1], recv_h.at[1], device
        ).start()
        remote(
            hid_ref.at[:, pl.ds(pl.multiple_of(to * COLS, 128), COLS)],
            hid_all.at[queue],
            send_h.at[0],
            recv_h.at[0],
            device,
        ).start()
        return carry

    lax.fori_loop(1, NQ, send_hidden, 0)
    pltpu.make_async_copy(hid_ref.at[:, own_columns(0)], hid_all.at[queue], recv_h.at[0]).start()

    wait_bytes(q_buf.at[y], recv_q.at[0])
    for d in (2, 1, 3):
        remote(
            q_buf.at[y],
            q_buf.at[y],
            send_y.at[d - 1],
            recv_y.at[d - 1],
            place(x, c, (y + d) % NY, z),
        ).start()

    for load in loads:
        load.wait()
    wait_bytes(act_all.at[pl.ds(0, NQ - 1)], recv_h.at[1])
    act = act_all[:, 0, :].astype(jnp.bfloat16)
    for n in range(3):
        consts[n] = jnp.dot(act, mod_buf[n], preferred_element_type=jnp.float32)
    consts[2] = 1.0 + consts[2]
    final32 = final_buf[...].astype(jnp.float32)
    for n in range(2):
        sums[n] = lax.dot_general(
            consts[2 - n],
            final32,
            (((1,), (1,)), ((), ())),
            preferred_element_type=jnp.float32,
            precision=lax.Precision.HIGHEST,
        )

    for blk in range(2):
        wait_bytes(kv.at[2 * x + blk], recv_kv.at[blk])
    for k in range(2):
        for side, to in ((0, xr), (1, xl)):
            blk = k if side == 0 else 1 - k
            remote(
                kv.at[2 * x + blk],
                kv.at[2 * x + blk],
                send_x.at[blk, side],
                recv_x.at[blk, side],
                place(to, c, y, z),
            ).start()

    def send_w(d, carry):
        remote(
            w_ref.at[:, own_columns(0)],
            w_all.at[z, y],
            send_w_ref.at[0],
            recv_wz.at[0],
            place(x, c, y, (z + d) % NZ),
        ).start()
        return carry

    lax.fori_loop(1, NZ, send_w, 0)
    pltpu.make_async_copy(w_ref.at[:, own_columns(0)], w_all.at[z, y], recv_wz.at[0]).start()

    for d in (1, 3, 2):
        wait_bytes(q_buf.at[(y + NY - d) % NY], recv_y.at[d - 1])

    lane = lax.broadcasted_iota(jnp.int32, (ROWS, 128), 1)
    row = lax.broadcasted_iota(jnp.int32, (ROWS, 128), 0)
    diagonal = lane == row
    stat_row = lax.broadcasted_iota(jnp.int32, (16, 128), 0)

    def finish(g, carry):
        total = acc[g, :, 128:]
        out = (acc[g, :, :128] / total).astype(jnp.bfloat16)
        level = peak[g] + jnp.log2(total)
        for part in range(NY):
            rows = slice(part * ROWS, (part + 1) * ROWS)
            vector = jnp.sum(jnp.where(diagonal, level[rows], 0.0), axis=0, keepdims=True)
            high = vector.astype(jnp.bfloat16).astype(jnp.float32)
            middle = (vector - high).astype(jnp.bfloat16).astype(jnp.float32)
            low = vector - high - middle
            stats = jnp.where(
                stat_row == 0,
                high,
                jnp.where(stat_row == 1, middle, jnp.where(stat_row == 2, low, 0.0)),
            )
            o_part[part, g, 0:ROWS] = out[rows]
            o_part[part, g, ROWS:] = stats.astype(jnp.bfloat16)
        return carry

    def partial_copy(half, d):
        to = (y + d) % NY
        rows = pl.ds(4 * half, 4)
        return remote(
            o_part.at[to, rows],
            o_recv.at[y, rows],
            send_o.at[half, d - 1],
            recv_o.at[half, d - 1],
            place(x, c, to, z),
        )

    key_rows = NZ * TOK

    def stage(st, carry):
        p = (x + st + st // 2 - 2 * (st // 3)) % NX

        @pl.when(st == 1)
        def _():
            wait_bytes(kv.at[2 * xl], recv_x.at[0, 0])
            remote(
                kv.at[2 * xl], kv.at[2 * xl], send_x.at[0, 2], recv_xr.at[0], place(xr, c, y, z)
            ).start()
            right = 2 * xr + 1
            wait_bytes(kv.at[right], recv_x.at[1, 1])
            remote(
                kv.at[right], kv.at[right], send_x.at[1, 2], recv_xr.at[1], place(xl, c, y, z)
            ).start()
            wait_bytes(kv.at[2 * xr], recv_x.at[0, 1])

        @pl.when(st == 2)
        def _():
            wait_bytes(w_all.at[:, y], recv_wz.at[0])
            for d in (1, 3, 2):
                remote(
                    w_all.at[:, y],
                    w_all.at[:, y],
                    send_w_ref.at[d],
                    recv_wy.at[d - 1],
                    place(x, c, (y + d) % NY, z),
                ).start()
            wait_bytes(kv.at[2 * xl + 1], recv_x.at[1, 0])

        @pl.when(st == 3)
        def _():
            wait_bytes(kv.at[2 * p], recv_xr.at[0])
            wait_bytes(kv.at[2 * p + 1], recv_xr.at[1])

        high, odd = p // 2, p % 2

        def both(i, carry):
            keys = kv[pl.ds(2 * p, 2), 0].reshape(2 * key_rows, DH)
            values = kv[pl.ds(2 * p, 2), 1].reshape(2 * key_rows, DH)
            attend(i, keys, values, q_buf, acc, peak)
            return carry

        def halves(half, carry):
            same = 1 - (high - half) * (high - half)
            count = 4 * high * (1 - half) + (2 * odd + 1) * same
            lax.fori_loop(4 * half, 4 * half + count, both, 0)

            @pl.when(high == half)
            def _():
                last = 2 * p + 1
                attend(
                    last,
                    kv[last, 0].reshape(key_rows, DH),
                    kv[last, 1].reshape(key_rows, DH),
                    q_buf,
                    acc,
                    peak,
                )

            @pl.when(st == 3)
            def _():
                lax.fori_loop(4 * half, 4 * half + 4, finish, 0)
                for d in (2, 1, 3):
                    partial_copy(half, d).start()

            return carry

        return lax.fori_loop(0, 2, halves, carry)

    lax.fori_loop(0, 4, stage, 0)

    def column(stats):
        stats = stats.astype(jnp.float32)
        vector = stats[0:1] + stats[1:2] + stats[2:3]
        return jnp.sum(
            jnp.where(diagonal, jnp.broadcast_to(vector, (ROWS, 128)), 0.0),
            axis=1,
            keepdims=True,
        )

    def merge(g, carry):
        parts = [o_part[y, g]] + [o_recv[(y + d) % NY, g] for d in (1, 2, 3)]
        levels = [column(part[ROWS:]) for part in parts]
        top = functools.reduce(jnp.maximum, levels)
        shares = [jnp.exp2(level - top) for level in levels]
        total = functools.reduce(jnp.add, shares)
        mixed = functools.reduce(
            jnp.add,
            [share * part[:ROWS].astype(jnp.float32) for share, part in zip(shares, parts)],
        )
        merged[g] = (mixed / total).astype(jnp.bfloat16).reshape(2, TOK, DH)
        for k in range(2):
            zt = (x + 8 - g) % 4 + 4 * k

            @pl.when(zt != z)
            def _():
                remote(
                    merged.at[g, k],
                    o_all.at[c, g, z],
                    send_z.at[0],
                    recv_z.at[g // 4],
                    place(x, c, y, zt),
                ).start()

            @pl.when(zt == z)
            def _():
                pltpu.make_async_copy(
                    merged.at[g, k], o_all.at[c, g, z], recv_z.at[g // 4]
                ).start()

        return carry

    def first(xs):
        return (xs + 8 - z) % 4

    def across(g, slot):
        return remote(
            o_all.at[c, g],
            o_all.at[c, g],
            send_c.at[slot],
            recv_c.at[slot],
            place(x, 1 - c, y, z),
        )

    for half in range(2):
        for d in (1, 3, 2):
            wait_bytes(
                o_recv.at[(y + NY - d) % NY, pl.ds(4 * half, 4)], recv_o.at[half, d - 1]
            )
        lax.fori_loop(4 * half, 4 * half + 4, merge, 0)
        g = first(x) + 4 * half
        wait_bytes(o_all.at[c, g], recv_z.at[half])
        for d in (2, 1, 3):
            remote(
                o_all.at[c, g],
                o_all.at[c, g],
                send_g.at[half, d - 1],
                recv_g.at[half, d - 1],
                place((x + d) % NX, c, y, z),
            ).start()
        across(g, 4 * half).start()

    wait_bytes(hid_all, recv_h.at[0])
    for d in (1, 2, 3):
        wait_bytes(w_all.at[:, (y + NY - d) % NY], recv_wy.at[d - 1])

    lat_lane = lax.broadcasted_iota(jnp.int32, (TOK, LAT), 1)
    for half in range(2):
        for d in (1, 3, 2):
            g = first((x + NX - d) % NX) + 4 * half
            wait_bytes(o_all.at[c, g], recv_g.at[half, d - 1])
            across(g, 4 * half + d).start()
        for d in range(NX):
            g = first((x + NX - d) % NX) + 4 * half
            wait_bytes(o_all.at[1 - c, g], recv_c.at[4 * half + d])

        projected = None
        for parity in range(NC):
            for zh in range(0, NZ, 2):
                left = jnp.concatenate(
                    [
                        o_all[parity, 4 * half : 4 * half + 4, zh + k].reshape(4 * TOK, DH)
                        for k in range(2)
                    ],
                    axis=1,
                )
                right = jnp.concatenate(
                    [w_all[zh + k, 2 * parity + n] for k in range(2) for n in range(2)], axis=0
                )
                term = jnp.dot(left, right, preferred_element_type=jnp.float32)
                projected = term if projected is None else projected + term

        for g in range(4 * half, 4 * half + 4):
            rows = slice((g % 4) * TOK, (g % 4 + 1) * TOK)
            stream = hid_all[g].astype(jnp.float32) + consts[0, g : g + 1, :] * projected[rows]
            center = jnp.mean(stream, axis=1, keepdims=True)
            apart = stream - center
            spread = jnp.sum(apart * apart, axis=1, keepdims=True)
            scaled = (apart * consts[2, g : g + 1, :]).astype(jnp.bfloat16)
            message[g, 0:TOK, 0:LAT] = lax.dot_general(
                scaled,
                final_buf[...],
                (((1,), (1,)), ((), ())),
                preferred_element_type=jnp.float32,
            )
            message[g, 0:TOK, LAT:] = jnp.where(
                lat_lane == 0, center, jnp.where(lat_lane == 1, spread, 0.0)
            )
            message[g, TOK:, 0:LAT] = jnp.broadcast_to(sums[0, g : g + 1, :], (8, LAT))
            message[g, TOK:, LAT:] = jnp.broadcast_to(sums[1, g : g + 1, :], (8, LAT))

            @pl.when(queue != g)
            def _():
                remote(
                    message.at[g],
                    received.at[queue],
                    send_m.at[g],
                    recv_m.at[queue],
                    {"queue": g, "seq": seq},
                ).start()

    blocks = [message[queue]]
    for d in range(1, NQ):
        source = (queue + NQ - d) % NQ
        wait_bytes(received.at[source], recv_m.at[source])
        blocks.append(received[source])
    centers = [block[0:TOK, LAT : LAT + 1] for block in blocks]
    center = functools.reduce(jnp.add, centers) / NQ
    summed = functools.reduce(jnp.add, [block[0:TOK, LAT + 1 : LAT + 2] for block in blocks])
    mixed = functools.reduce(jnp.add, [block[0:TOK, 0:LAT] for block in blocks])
    offset = functools.reduce(jnp.add, [block[TOK : TOK + 1, LAT:] for block in blocks])
    for block, local in zip(blocks, centers):
        away = local - center
        summed = summed + COLS * (away * away)
        mixed = mixed + away * block[TOK : TOK + 1, 0:LAT]
    velocity = mixed / jnp.sqrt(summed / D + 1e-06) + offset
    update[:, 0:LAT] = lat_buf[...] - STRIDE / 1000.0 * velocity
    update[:, LAT:] = velocity
    behind = remote(
        update,
        arrived,
        move_sem.at[0],
        move_sem.at[1],
        {"queue": (queue + 1) % NQ, "seq": seq},
    )
    behind.start()
    out_ref[:, 0:LAT] = velocity

    wait_bytes(hid_all.at[pl.ds(0, NQ - 1)], send_h.at[0])
    wait_bytes(act_all.at[pl.ds(0, NQ - 1)], send_h.at[1])
    wait_bytes(q_buf.at[pl.ds(0, 3), pl.ds(0, 5)], send_a.at[0])
    wait_bytes(q_buf.at[pl.ds(0, 3), pl.ds(0, 5), 0], send_a.at[1])

    @pl.when(xt != x)
    def _():
        wait_bytes(q_buf.at[0, 0, 0], send_a.at[2])

    wait_bytes(w_all.at[pl.ds(0, NZ - 1), 0], send_w_ref.at[0])
    for blk in range(2):
        for side in range(3):
            wait_bytes(kv.at[0], send_x.at[blk, side])
    for d in (1, 2, 3):
        wait_bytes(q_buf.at[0], send_y.at[d - 1])
        wait_bytes(w_all.at[:, 0], send_w_ref.at[d])
        for half in range(2):
            wait_bytes(o_part.at[0, pl.ds(0, 4)], send_o.at[half, d - 1])
            wait_bytes(o_all.at[0, 0], send_g.at[half, d - 1])
    wait_bytes(merged.at[pl.ds(0, 7)], send_z.at[0])
    for slot in range(8):
        wait_bytes(o_all.at[0, 0], send_c.at[slot])
    for g in range(NQ):

        @pl.when(queue != g)
        def _():
            wait_bytes(message.at[0], send_m.at[g])

    behind.wait_recv()
    out_ref[:, LAT:] = jnp.where(queue == 0, fresh_buf[...], arrived[:, 0:LAT])
    behind.wait_send()


def fused(*operands):
    bf16, f32 = jnp.bfloat16, jnp.float32
    vmem, dma = pltpu.VMEM, pltpu.SemaphoreType.DMA
    in_specs = [pl.BlockSpec(memory_space=pl.ANY)] * 10
    in_specs[5] = pl.BlockSpec(memory_space=pltpu.SMEM)
    return pl.pallas_call(
        fused_kernel,
        out_shape=jax.ShapeDtypeStruct((TOK, 2 * LAT), f32),
        in_specs=in_specs,
        out_specs=pl.BlockSpec(memory_space=pltpu.VMEM),
        scratch_shapes=[
            vmem((NQ, 2, NZ, TOK, DH), bf16),
            vmem((NY, NQ, 2, TOK, DH), bf16),
            vmem((NQ, NY * ROWS, 256), f32),
            vmem((NQ, NY * ROWS, 128), f32),
            vmem((NY, NQ, PART, DH), bf16),
            vmem((NY, NQ, PART, DH), bf16),
            vmem((NQ, 2, TOK, DH), bf16),
            vmem((NC, NQ, NZ, TOK, DH), bf16),
            vmem((NQ, TOK, COLS), bf16),
            vmem((NQ, 8, TEMB), f32),
            vmem((NZ, NY, 64, COLS), bf16),
            vmem((3, TEMB, COLS), bf16),
            vmem((LAT, COLS), bf16),
            vmem((TOK, LAT), f32),
            vmem((TOK, LAT), f32),
            vmem((3, NQ, COLS), f32),
            vmem((2, NQ, LAT), f32),
            vmem((NQ, TOK + 8, 128), f32),
            vmem((NQ, TOK + 8, 128), f32),
            vmem((TOK, 128), f32),
            vmem((TOK, 128), f32),
            dma((6,)),
            dma((3,)),
            dma((2,)),
            dma((4,)),
            dma((2, 3)),
            dma((3,)),
            dma((2, 3)),
            dma((1,)),
            dma((2, 3)),
            dma((8,)),
            dma((NQ,)),
            dma((2,)),
            dma((1,)),
            dma((2,)),
            dma((1,)),
            dma((3,)),
            dma((2, 2)),
            dma((2,)),
            dma((3,)),
            dma((2, 3)),
            dma((2,)),
            dma((2, 3)),
            dma((8,)),
            dma((NQ,)),
            dma((2,)),
        ],
        compiler_params=pltpu.CompilerParams(
            collective_id=0, has_side_effects=True, vmem_limit_bytes=60 * 1024 * 1024
        ),
        name="fused",
    )(*operands)


def body(
    hidden,
    queries,
    keys,
    values,
    timesteps,
    latents,
    fresh_noise,
    out_weight,
    mod_weight,
    final_weight,
):
    result = fused(
        queries[0],
        keys[0],
        values[0],
        hidden[0],
        out_weight,
        timesteps,
        mod_weight,
        final_weight.T,
        latents[0],
        fresh_noise,
    )
    return result[None, :, :LAT], result[None, :, LAT:]


def solution(mesh):
    placed = (
        P("queue", "seq", None),
        P("queue", "seq", None),
        P("queue", "seq", None),
        P("queue", "seq", None),
        P("queue"),
        P("queue", "seq", None),
        P("seq", None),
        P("seq", None),
        P(),
        P(),
    )
    return jax.shard_map(
        body,
        mesh=mesh,
        in_specs=placed,
        out_specs=(P("queue", "seq", None), P("queue", "seq", None)),
        check_vma=False,
    )
```

time: 232 us -> 99.6 us (0.43)
  Pallas kernels: 0 us -> 94.9 us
  waiting for transfers between devices: 82.7 us -> 0 us
  matrix products: 69.3 us -> 0 us
  blocking collectives: 32.1 us -> 0 us
  starting transfers between devices: 16.6 us -> 0 us
  between operations: 14.9 us -> 1.29 us
  other arithmetic: 11.4 us -> 0 us
    pallas_call x0 -> x1, Pallas kernels: none -> 94.9 us  [fused(): pl.pallas_call(fused_kernel, out_shape=jax.ShapeDtypeStruct((TOK, 2 * LAT...]
    dot_general x15 -> x0, matrix products: 69.3 us -> none  [the longest x6 29.8 us: fold_block(): jnp.einsum('hqk,khd->hqd', weights.astype(jnp.bfloat16), value_part, pref...]
    all_gather x2 -> x0, waiting for transfers between devices: 61.4 us -> none  [the longest x1 37.8 us: body(): lax.all_gather(out_weight, 'seq', axis=0, tiled=True)]
    all_to_all x1 -> x0, blocking collectives: 32.1 us -> none  [body(): lax.all_to_all(paired, 'seq', split_axis=1, concat_axis=2, tiled=True)]
    all_to_all x2 -> x0, waiting for transfers between devices: 18.5 us -> none  [the longest x1 9.41 us: body(): lax.all_to_all(attended, 'seq', split_axis=0, concat_axis=2, tiled=True)]
    all_to_all x2 -> x0, starting transfers between devices: 15.3 us -> none  [the longest x1 9.51 us: body(): lax.all_to_all(attended, 'seq', split_axis=0, concat_axis=2, tiled=True)]
    reduce_sum x7 -> x0, other arithmetic: 8.26 us -> none  [the longest x6 8.02 us: fold_block(): new_total = running_total * factor + jnp.sum(weights, axis=2)]
  transfers between devices with their start and end apart: 5 -> 0, of which waited for: 5 -> 0; matrix products, arithmetic and copies ran while one was open for 31% -> 0% of each run, Pallas kernels for 0% -> 0%
where the time goes in v2:
time: 99.6 us; the launch traced here: 97.7 us
  Pallas kernels  94.9 us (95%)
  local copies, waits for them, and re-layouts  1.5 us (2%)
  between operations  1.29 us (1%)
    pallas_call x1, Pallas kernels, fused(): pl.pallas_call(fused_kernel, out_shape=jax.ShapeDtypeStruct((TOK, 2 * LAT...  94.9 us

profile of v2, /device:TPU:7, one launch (start us, length us, event | category | flops | bytes accessed | tf_op | source)
XLA Modules:
  0.0 97.7 jit_solution(8004135384619972650)
XLA Ops:
  1.3 94.9 %fused.1 = f32[48,128]{1,0:T(8,128)} custom-call(bf16[48,2048]{1,0:T(8,128)(2,1)} %bitcast.12, bf16[48,2048]{1,0:T(8,128)(2,1)} %bitcast.13, bf16[48,2048]{1,0:T(8,128)(2,1)} %bitcast.14, bf16[48,3072]{1,0:T(8,128)(2,1)} %bitcast.11, bf16[64,3072]{1,0:T(8,128)(2,1)} %w_ref.1, s32[1]{0:T(128)S(6)} %copy.12.step_ref, bf16[256,9216]{1,0:T(8,128)(2,1)} %mod_ref.1, ...), custom_call_target="tpu_custom_call" | custom-call | tf_op jit(solution)/shard_map/fused/pallas_call | solution.py:596
  96.2 1.5 %slice_bitcast_fusion = (f32[1,48,64]{2,1,0:T(8,128)}, f32[1,48,64]{2,1,0:T(8,128)}) fusion(f32[48,128]{1,0:T(8,128)} %fused.1), kind=kLoop, calls=%fused_computation | loop fusion | bytes 49152 | tf_op jit(solution)/shard_map/broadcast_in_dim | solution.py:680

commit v3 on v2

v3 whole, which is shorter than its diff:
```python
import functools
import math

import jax
import jax.numpy as jnp
from jax import lax
from jax.experimental import pallas as pl
from jax.experimental.pallas import tpu as pltpu
from jax.sharding import PartitionSpec as P

D = 3072
H = 16
DH = 128
TEMB = 256
STRIDE = 125
NX, NC, NY, NZ = 4, 2, 4, 8
NQ = NX * NC
TOK = 48
COLS = D // NQ
LAT = 64
ROWS = 2 * TOK
PART = 4 * ROWS + 16
MSG = TOK // 2 + 8
SCALE = DH**-0.5 * math.log2(math.e)
MESH = pl.DeviceIdType.MESH


def place(x, c, y, z):
    return {"queue": x * NC + c, "seq": z * NY + y}


def remote(src, dst, send_sem, recv_sem, device):
    return pltpu.make_async_remote_copy(
        src_ref=src,
        dst_ref=dst,
        send_sem=send_sem,
        recv_sem=recv_sem,
        device_id=device,
        device_id_type=MESH,
    )


def wait_bytes(ref, sem):
    pltpu.make_async_copy(ref, ref, sem).wait()


def attend(i, keys, values, q_buf, acc, peak):
    count = keys.shape[0]
    query = q_buf[:, i].reshape(NY * 2 * TOK, DH)
    extended = jnp.concatenate([values, jnp.ones_like(values)], axis=1)
    for part in range(3):
        rows = slice(part * 128, part * 128 + 128)
        scores = (
            lax.dot_general(
                query[rows], keys, (((1,), (1,)), ((), ())), preferred_element_type=jnp.float32
            )
            * SCALE
        )
        old = peak[i, rows, :]
        new = jnp.maximum(old, jnp.max(scores, axis=1, keepdims=True))
        factor = jnp.exp2(old - new)
        weights = jnp.exp2(scores - jnp.concatenate([new] * (count // 128), axis=1))
        mixed = jnp.dot(
            weights.astype(jnp.bfloat16), extended, preferred_element_type=jnp.float32
        )
        acc[i, rows, :] = acc[i, rows, :] * jnp.concatenate([factor, factor], axis=1) + mixed
        peak[i, rows, :] = new


def fused_kernel(
    q_ref,
    k_ref,
    v_ref,
    hid_ref,
    w_ref,
    step_ref,
    mod_ref,
    final_ref,
    lat_ref,
    fresh_ref,
    out_ref,
    k_buf,
    v_buf,
    q_buf,
    acc,
    peak,
    o_part,
    o_recv,
    merged,
    o_all,
    hid_all,
    act_all,
    w_all,
    mod_buf,
    final_buf,
    lat_behind,
    fresh_buf,
    consts,
    sums,
    message,
    received,
    load_sem,
    send_a,
    send_h,
    send_wy,
    send_wz,
    send_x,
    send_y,
    send_o,
    send_z,
    send_g,
    send_c,
    send_m,
    recv_k,
    recv_v,
    recv_q,
    recv_h,
    recv_wy,
    recv_wz,
    recv_x,
    recv_y,
    recv_o,
    recv_z,
    recv_g,
    recv_c,
    recv_m,
):
    queue = lax.axis_index("queue")
    seq = lax.axis_index("seq")
    x, c = queue // NC, queue % NC
    z, y = seq // NY, seq % NY
    xl, xr, x2 = (x + NX - 1) % NX, (x + 1) % NX, (x + 2) % NX
    yl, yr, y2 = (y + NY - 1) % NY, (y + 1) % NY, (y + 2) % NY
    zl, zr = (z + NZ - 1) % NZ, (z + 1) % NZ
    zk = z // 4
    xt = (z + queue) % NX
    own_head = 2 * z + c
    barrier = pltpu.get_barrier_semaphore()

    def greet(j, carry):
        device = place((x + j // 16) % NX, (c + j % 2) % NC, y, (z + (j // 2) % 8) % NZ)
        pl.semaphore_signal(barrier, inc=1, device_id=device, device_id_type=MESH)
        return carry

    lax.fori_loop(1, 64, greet, 0)
    for d in (1, 2, 3):
        pl.semaphore_signal(
            barrier, inc=1, device_id=place(x, c, (y + d) % NY, z), device_id_type=MESH
        )

    def own_columns(part):
        return pl.ds(pl.multiple_of(part * D + queue * COLS, 128), COLS)

    loads = [
        pltpu.make_async_copy(mod_ref.at[:, own_columns(n)], mod_buf.at[n], load_sem.at[n])
        for n in range(3)
    ]
    loads.append(pltpu.make_async_copy(final_ref.at[:, own_columns(0)], final_buf, load_sem.at[3]))
    loads.append(pltpu.make_async_copy(fresh_ref, fresh_buf, load_sem.at[4]))
    for load in loads:
        load.start()

    pl.semaphore_wait(barrier, 66)

    def columns(ref, head):
        return ref.at[:, pl.ds(pl.multiple_of(head * DH, DH), DH)]

    def by_head(array, ref, target, sem, xs):
        def send(j, carry):
            zt, ct = (z + j // 2) % NZ, (c + j % 2) % NC
            remote(
                columns(ref, 2 * zt + ct), target, send_a.at[array], sem, place(xs, ct, y, zt)
            ).start()
            return carry

        lax.fori_loop(1, 16, send, 0)

    by_head(0, k_ref, k_buf.at[queue, z], recv_k.at[c], x)
    pltpu.make_async_copy(columns(k_ref, own_head), k_buf.at[queue, z], recv_k.at[c]).start()
    by_head(1, q_ref, q_buf.at[y, queue, zk], recv_q.at[0], xt)

    @pl.when(xt != x)
    def _():
        remote(
            columns(q_ref, own_head),
            q_buf.at[y, queue, zk],
            send_a.at[3],
            recv_q.at[0],
            place(xt, c, y, z),
        ).start()

    @pl.when(xt == x)
    def _():
        pltpu.make_async_copy(
            columns(q_ref, own_head), q_buf.at[y, queue, zk], recv_q.at[0]
        ).start()

    by_head(2, v_ref, v_buf.at[queue, z], recv_v.at[c], x)
    pltpu.make_async_copy(columns(v_ref, own_head), v_buf.at[queue, z], recv_v.at[c]).start()

    for d in (1, 2, 3):
        remote(
            w_ref.at[:, own_columns(0)],
            w_all.at[z, y],
            send_wy.at[d - 1],
            recv_wy.at[0],
            place(x, c, (y + d) % NY, z),
        ).start()
    pltpu.make_async_copy(w_ref.at[:, own_columns(0)], w_all.at[z, y], recv_wy.at[0]).start()

    halfway = TEMB // 2
    index = lax.broadcasted_iota(jnp.int32, (8, halfway), 1).astype(jnp.float32)
    angles = step_ref[0].astype(jnp.float32) * jnp.exp(-math.log(10000.0) * index / halfway)
    embed = jnp.concatenate([jnp.cos(angles), jnp.sin(angles)], axis=1)
    act_all[queue] = embed / (1.0 + jnp.exp(-embed))

    def send_hidden(d, carry):
        to = (queue + d) % NQ
        device = {"queue": to, "seq": seq}
        remote(
            act_all.at[queue], act_all.at[queue], send_h.at[1], recv_h.at[1], device
        ).start()
        remote(
            hid_ref.at[:, pl.ds(pl.multiple_of(to * COLS, 128), COLS)],
            hid_all.at[queue],
            send_h.at[0],
            recv_h.at[0],
            device,
        ).start()
        return carry

    lax.fori_loop(1, NQ, send_hidden, 0)
    pltpu.make_async_copy(hid_ref.at[:, own_columns(0)], hid_all.at[queue], recv_h.at[0]).start()

    @pl.when(queue < NQ - 1)
    def _():
        remote(
            lat_ref,
            lat_behind,
            send_h.at[2],
            recv_h.at[2],
            {"queue": (queue + 1) % NQ, "seq": seq},
        ).start()

    acc[...] = jnp.zeros_like(acc)
    peak[...] = jnp.full_like(peak, -1e30)

    def along_x(array, ref):
        for n in range(2):
            for side, to in ((0, xr), (1, xl)):
                blk = n if side == 0 else 1 - n
                block = ref.at[2 * x + blk]
                remote(
                    block,
                    block,
                    send_x.at[array, side, blk],
                    recv_x.at[array, side, blk],
                    place(to, c, y, z),
                ).start()

    def relay_x(array, ref):
        for side, source, to in ((0, xl, xr), (1, xr, xl)):
            block = ref.at[2 * source + side]
            wait_bytes(block, recv_x.at[array, side, side])
            remote(
                block,
                block,
                send_x.at[array, side, 2],
                recv_x.at[array, side, 2],
                place(to, c, y, z),
            ).start()

    for blk in range(2):
        wait_bytes(k_buf.at[2 * x + blk], recv_k.at[blk])
    along_x(0, k_buf)

    wait_bytes(q_buf.at[y], recv_q.at[0])
    for side, to in ((0, yr), (1, yl)):
        remote(
            q_buf.at[y], q_buf.at[y], send_y.at[side, 0], recv_y.at[side, 0], place(x, c, to, z)
        ).start()

    for load in loads:
        load.wait()
    wait_bytes(act_all.at[pl.ds(0, NQ - 1)], recv_h.at[1])
    act = act_all[:, 0, :].astype(jnp.bfloat16)
    for n in range(3):
        consts[n] = jnp.dot(act, mod_buf[n], preferred_element_type=jnp.float32)
    consts[2] = 1.0 + consts[2]
    final32 = final_buf[...].astype(jnp.float32)
    for n in range(2):
        sums[n] = lax.dot_general(
            consts[2 - n],
            final32,
            (((1,), (1,)), ((), ())),
            preferred_element_type=jnp.float32,
            precision=lax.Precision.HIGHEST,
        )

    relay_x(0, k_buf)
    for blk in range(2):
        wait_bytes(v_buf.at[2 * x + blk], recv_v.at[blk])
    along_x(1, v_buf)
    for side, source, to in ((0, yl, yr), (1, yr, yl)):
        wait_bytes(q_buf.at[source], recv_y.at[side, 0])
        slab = q_buf.at[source, pl.ds(4 * side, 4)]
        remote(
            slab, slab, send_y.at[side, 1], recv_y.at[side, 1], place(x, c, to, z)
        ).start()

    def ring_z(step):
        for side, to in ((0, zr), (1, zl)):
            back = NZ - step if side == 0 else step
            rows = pl.ds(0, NY) if step < 3 else pl.ds(2 * side, 2)
            chunk = w_all.at[(z + back) % NZ]
            if step:
                wait_bytes(chunk, recv_wz.at[side, step - 1])
            chunk = w_all.at[(z + back) % NZ, rows]
            remote(
                chunk,
                chunk,
                send_wz.at[side, step],
                recv_wz.at[side, step],
                place(x, c, y, to),
            ).start()

    wait_bytes(w_all.at[z], recv_wy.at[0])
    ring_z(0)
    for side in range(2):
        wait_bytes(q_buf.at[y2, pl.ds(4 * side, 4)], recv_y.at[side, 1])

    lane = lax.broadcasted_iota(jnp.int32, (ROWS, 128), 1)
    row = lax.broadcasted_iota(jnp.int32, (ROWS, 128), 0)
    diagonal = lane == row
    stat_row = lax.broadcasted_iota(jnp.int32, (16, 128), 0)

    def finish(half):
        vectors = [[] for _ in range(NY)]
        for k in range(4):
            g = 4 * half + k
            total = acc[g, :, 128:]
            out = (acc[g, :, :128] / total).astype(jnp.bfloat16)
            level = peak[g] + jnp.log2(total)
            for part in range(NY):
                rows = slice(part * ROWS, (part + 1) * ROWS)
                vector = jnp.sum(jnp.where(diagonal, level[rows], 0.0), axis=0, keepdims=True)
                high = vector.astype(jnp.bfloat16).astype(jnp.float32)
                middle = (vector - high).astype(jnp.bfloat16).astype(jnp.float32)
                vectors[part] += [high, middle, vector - high - middle]
                o_part[part, half, k * ROWS : (k + 1) * ROWS] = out[rows]
        for part in range(NY):
            stats = jnp.zeros((16, 128), jnp.float32)
            for n, vector in enumerate(vectors[part]):
                stats = jnp.where(stat_row == n, vector, stats)
            o_part[part, half, 4 * ROWS :] = stats.astype(jnp.bfloat16)

    def partial_copy(half, d):
        to = (y + d) % NY
        return remote(
            o_part.at[to, half],
            o_recv.at[y, half],
            send_o.at[half, d - 1],
            recv_o.at[half, d - 1],
            place(x, c, to, z),
        )

    key_rows = NZ * TOK

    def stage(st, carry):
        p = (x + st + st // 2 - 2 * (st // 3)) % NX

        @pl.when(st == 1)
        def _():
            relay_x(1, v_buf)
            for ref, array in ((k_buf, 0), (v_buf, 1)):
                wait_bytes(ref.at[2 * xr], recv_x.at[array, 1, 0])

        @pl.when(st == 2)
        def _():
            ring_z(1)
            for ref, array in ((k_buf, 0), (v_buf, 1)):
                wait_bytes(ref.at[2 * xl + 1], recv_x.at[array, 0, 1])

        @pl.when(st == 3)
        def _():
            for ref, array in ((k_buf, 0), (v_buf, 1)):
                for side in range(2):
                    wait_bytes(ref.at[2 * x2 + side], recv_x.at[array, side, 2])

        high, odd = p // 2, p % 2

        def both(i, carry):
            keys = k_buf[pl.ds(2 * p, 2)].reshape(2 * key_rows, DH)
            values = v_buf[pl.ds(2 * p, 2)].reshape(2 * key_rows, DH)
            attend(i, keys, values, q_buf, acc, peak)
            return carry

        def halves(half, carry):
            same = 1 - (high - half) * (high - half)
            count = 4 * high * (1 - half) + (2 * odd + 1) * same
            lax.fori_loop(4 * half, 4 * half + count, both, 0)

            @pl.when(high == half)
            def _():
                last = 2 * p + 1
                attend(
                    last,
                    k_buf[last].reshape(key_rows, DH),
                    v_buf[last].reshape(key_rows, DH),
                    q_buf,
                    acc,
                    peak,
                )

            @pl.when(st == 3)
            def _():
                finish(half)
                for d in (2, 1, 3):
                    partial_copy(half, d).start()

            return carry

        return lax.fori_loop(0, 2, halves, carry)

    lax.fori_loop(0, 4, stage, 0)
    ring_z(2)

    def column(vector):
        return jnp.sum(
            jnp.where(diagonal, jnp.broadcast_to(vector, (ROWS, 128)), 0.0),
            axis=1,
            keepdims=True,
        )

    def merge(half):
        refs = [o_part.at[y, half]] + [o_recv.at[(y + d) % NY, half] for d in (1, 2, 3)]
        stats = [ref[4 * ROWS :].astype(jnp.float32) for ref in refs]
        for k in range(4):
            g = 4 * half + k
            levels = [
                column(stat[3 * k : 3 * k + 1] + stat[3 * k + 1 : 3 * k + 2] + stat[3 * k + 2 : 3 * k + 3])
                for stat in stats
            ]
            top = functools.reduce(jnp.maximum, levels)
            shares = [jnp.exp2(level - top) for level in levels]
            total = functools.reduce(jnp.add, shares)
            mixed = functools.reduce(
                jnp.add,
                [
                    share * ref[k * ROWS : (k + 1) * ROWS].astype(jnp.float32)
                    for share, ref in zip(shares, refs)
                ],
            )
            merged[g] = (mixed / total).astype(jnp.bfloat16).reshape(2, TOK, DH)
            for n in range(2):
                zt = (x + 8 - g) % 4 + 4 * n

                @pl.when(zt != z)
                def _():
                    remote(
                        merged.at[g, n],
                        o_all.at[c, g, z],
                        send_z.at[0],
                        recv_z.at[half],
                        place(x, c, y, zt),
                    ).start()

                @pl.when(zt == z)
                def _():
                    pltpu.make_async_copy(
                        merged.at[g, n], o_all.at[c, g, z], recv_z.at[half]
                    ).start()

    def first(xs):
        return (xs + 8 - z) % 4

    def across(g, slot):
        return remote(
            o_all.at[c, g],
            o_all.at[c, g],
            send_c.at[slot],
            recv_c.at[slot],
            place(x, 1 - c, y, z),
        )

    for half in range(2):
        for d in (1, 3, 2):
            wait_bytes(o_recv.at[(y + NY - d) % NY, half], recv_o.at[half, d - 1])
        merge(half)
        g = first(x) + 4 * half
        wait_bytes(o_all.at[c, g], recv_z.at[half])
        for d in (2, 1, 3):
            remote(
                o_all.at[c, g],
                o_all.at[c, g],
                send_g.at[half, d - 1],
                recv_g.at[half, d - 1],
                place((x + d) % NX, c, y, z),
            ).start()
        across(g, 4 * half).start()
        if half == 0:
            ring_z(3)

    wait_bytes(hid_all, recv_h.at[0])
    for side in range(2):
        wait_bytes(w_all.at[(z + 4) % NZ, pl.ds(2 * side, 2)], recv_wz.at[side, 3])

    token_lane = lax.broadcasted_iota(jnp.int32, (TOK, 128), 1)
    token_row = lax.broadcasted_iota(jnp.int32, (TOK, 128), 0)
    token_diagonal = token_lane == token_row
    last_row = lax.broadcasted_iota(jnp.int32, (8, 128), 0)

    def as_row(vector):
        return jnp.sum(
            jnp.where(token_diagonal, jnp.broadcast_to(vector, (TOK, 128)), 0.0),
            axis=0,
            keepdims=True,
        )

    def as_column(vector):
        return jnp.sum(
            jnp.where(token_diagonal, jnp.broadcast_to(vector, (TOK, 128)), 0.0),
            axis=1,
            keepdims=True,
        )

    for half in range(2):
        for d in (1, 3, 2):
            g = first((x + NX - d) % NX) + 4 * half
            wait_bytes(o_all.at[c, g], recv_g.at[half, d - 1])
            across(g, 4 * half + d).start()
        for d in range(NX):
            g = first((x + NX - d) % NX) + 4 * half
            wait_bytes(o_all.at[1 - c, g], recv_c.at[4 * half + d])

        projected = None
        for parity in range(NC):
            for zh in range(0, NZ, 2):
                left = jnp.concatenate(
                    [
                        o_all[parity, 4 * half : 4 * half + 4, zh + k].reshape(4 * TOK, DH)
                        for k in range(2)
                    ],
                    axis=1,
                )
                right = jnp.concatenate(
                    [w_all[zh + k, 2 * parity + n] for k in range(2) for n in range(2)], axis=0
                )
                term = jnp.dot(left, right, preferred_element_type=jnp.float32)
                projected = term if projected is None else projected + term

        for g in range(4 * half, 4 * half + 4):
            rows = slice((g % 4) * TOK, (g % 4 + 1) * TOK)
            stream = hid_all[g].astype(jnp.float32) + consts[0, g : g + 1, :] * projected[rows]
            center = jnp.mean(stream, axis=1, keepdims=True)
            apart = stream - center
            spread = jnp.sum(apart * apart, axis=1, keepdims=True)
            scaled = (apart * consts[2, g : g + 1, :]).astype(jnp.bfloat16)
            mixed = lax.dot_general(
                scaled,
                final_buf[...],
                (((1,), (1,)), ((), ())),
                preferred_element_type=jnp.float32,
            )
            message[g, 0 : TOK // 2] = jnp.concatenate(
                [mixed[: TOK // 2], mixed[TOK // 2 :]], axis=1
            )
            both_sums = jnp.concatenate([sums[0, g : g + 1], sums[1, g : g + 1]], axis=1)
            message[g, TOK // 2 :] = jnp.where(
                last_row == 0,
                as_row(center),
                jnp.where(last_row == 1, as_row(spread), both_sums),
            )
            for later in range(2 if g < NQ - 1 else 1):

                @pl.when(queue != g + later)
                def _():
                    remote(
                        message.at[g],
                        received.at[later, queue],
                        send_m.at[later, g],
                        recv_m.at[later, queue],
                        {"queue": g + later, "seq": seq},
                    ).start()

                @pl.when(queue == g + later)
                def _():
                    pltpu.make_async_copy(
                        message.at[g], received.at[later, queue], recv_m.at[later, queue]
                    ).start()

    def velocity_of(later):
        for source in range(NQ):
            wait_bytes(received.at[later, source], recv_m.at[later, source])
        tails = [received[later, source, TOK // 2 :] for source in range(NQ)]
        center = functools.reduce(jnp.add, [tail[0:1] for tail in tails]) / NQ
        spread = functools.reduce(jnp.add, [tail[1:2] for tail in tails])
        mixed = functools.reduce(
            jnp.add, [received[later, source, : TOK // 2] for source in range(NQ)]
        )
        mixed = jnp.concatenate([mixed[:, :LAT], mixed[:, LAT:]], axis=0)
        offset = functools.reduce(jnp.add, [tail[2:3, LAT:] for tail in tails])
        for tail in tails:
            away = tail[0:1] - center
            spread = spread + COLS * (away * away)
            mixed = mixed + as_column(away) * tail[2:3, :LAT]
        return mixed * as_column(1.0 / jnp.sqrt(spread / D + 1e-06)) + offset

    wait_bytes(hid_all.at[pl.ds(0, NQ - 1)], send_h.at[0])
    wait_bytes(act_all.at[pl.ds(0, NQ - 1)], send_h.at[1])
    for array in range(3):
        wait_bytes(q_buf.at[pl.ds(0, 3), pl.ds(0, 5), 0], send_a.at[array])

    @pl.when(xt != x)
    def _():
        wait_bytes(q_buf.at[0, 0, 0], send_a.at[3])

    @pl.when(queue < NQ - 1)
    def _():
        wait_bytes(lat_behind, send_h.at[2])

    for d in range(3):
        wait_bytes(w_all.at[0, 0], send_wy.at[d])
    for side in range(2):
        for array in range(2):
            for n in range(3):
                wait_bytes(k_buf.at[0], send_x.at[array, side, n])
        wait_bytes(q_buf.at[0], send_y.at[side, 0])
        wait_bytes(q_buf.at[0, pl.ds(0, 4)], send_y.at[side, 1])
        for step in range(4):
            wait_bytes(w_all.at[0, pl.ds(0, NY if step < 3 else 2)], send_wz.at[side, step])
    for d in (1, 2, 3):
        for half in range(2):
            wait_bytes(o_part.at[0, 0], send_o.at[half, d - 1])
            wait_bytes(o_all.at[0, 0], send_g.at[half, d - 1])
    wait_bytes(merged.at[pl.ds(0, 7)], send_z.at[0])
    for slot in range(8):
        wait_bytes(o_all.at[0, 0], send_c.at[slot])
    for g in range(NQ):
        for later in range(2 if g < NQ - 1 else 1):

            @pl.when(queue != g + later)
            def _():
                wait_bytes(message.at[0], send_m.at[later, g])

    out_ref[:, 0:LAT] = velocity_of(0)

    @pl.when(queue == 0)
    def _():
        out_ref[:, LAT:] = fresh_buf[...]

    @pl.when(queue > 0)
    def _():
        velocity = velocity_of(1)
        wait_bytes(lat_behind, recv_h.at[2])
        out_ref[:, LAT:] = lat_behind[...] - STRIDE / 1000.0 * velocity


def fused(*operands):
    bf16, f32 = jnp.bfloat16, jnp.float32
    vmem, dma = pltpu.VMEM, pltpu.SemaphoreType.DMA
    in_specs = [pl.BlockSpec(memory_space=pl.ANY)] * 10
    in_specs[5] = pl.BlockSpec(memory_space=pltpu.SMEM)
    return pl.pallas_call(
        fused_kernel,
        out_shape=jax.ShapeDtypeStruct((TOK, 2 * LAT), f32),
        in_specs=in_specs,
        out_specs=pl.BlockSpec(memory_space=pltpu.VMEM),
        scratch_shapes=[
            vmem((NQ, NZ, TOK, DH), bf16),
            vmem((NQ, NZ, TOK, DH), bf16),
            vmem((NY, NQ, 2, TOK, DH), bf16),
            vmem((NQ, NY * ROWS, 256), f32),
            vmem((NQ, NY * ROWS, 128), f32),
            vmem((NY, 2, PART, DH), bf16),
            vmem((NY, 2, PART, DH), bf16),
            vmem((NQ, 2, TOK, DH), bf16),
            vmem((NC, NQ, NZ, TOK, DH), bf16),
            vmem((NQ, TOK, COLS), bf16),
            vmem((NQ, 8, TEMB), f32),
            vmem((NZ, NY, 64, COLS), bf16),
            vmem((3, TEMB, COLS), bf16),
            vmem((LAT, COLS), bf16),
            vmem((TOK, LAT), f32),
            vmem((TOK, LAT), f32),
            vmem((3, NQ, COLS), f32),
            vmem((2, NQ, LAT), f32),
            vmem((NQ, MSG, 128), f32),
            vmem((2, NQ, MSG, 128), f32),
            dma((5,)),
            dma((4,)),
            dma((3,)),
            dma((3,)),
            dma((2, 4)),
            dma((2, 2, 3)),
            dma((2, 2)),
            dma((2, 3)),
            dma((1,)),
            dma((2, 3)),
            dma((8,)),
            dma((2, NQ)),
            dma((2,)),
            dma((2,)),
            dma((1,)),
            dma((3,)),
            dma((1,)),
            dma((2, 4)),
            dma((2, 2, 3)),
            dma((2, 2)),
            dma((2, 3)),
            dma((2,)),
            dma((2, 3)),
            dma((8,)),
            dma((2, NQ)),
        ],
        compiler_params=pltpu.CompilerParams(
            collective_id=0, has_side_effects=True, vmem_limit_bytes=60 * 1024 * 1024
        ),
        name="fused",
    )(*operands)


def body(
    hidden,
    queries,
    keys,
    values,
    timesteps,
    latents,
    fresh_noise,
    out_weight,
    mod_weight,
    final_weight,
):
    result = fused(
        queries[0],
        keys[0],
        values[0],
        hidden[0],
        out_weight,
        timesteps,
        mod_weight,
        final_weight.T,
        latents[0],
        fresh_noise,
    )
    return result[None, :, :LAT], result[None, :, LAT:]


def solution(mesh):
    placed = (
        P("queue", "seq", None),
        P("queue", "seq", None),
        P("queue", "seq", None),
        P("queue", "seq", None),
        P("queue"),
        P("queue", "seq", None),
        P("seq", None),
        P("seq", None),
        P(),
        P(),
    )
    return jax.shard_map(
        body,
        mesh=mesh,
        in_specs=placed,
        out_specs=(P("queue", "seq", None), P("queue", "seq", None)),
        check_vma=False,
    )
```

time: 99.6 us -> 88.1 us (0.88); the launches traced: 97.7 us -> 87.7 us
  Pallas kernels: 94.9 us -> 84.9 us
    pallas_call x1, Pallas kernels: 94.9 us -> 84.9 us  [fused(): pl.pallas_call(fused_kernel, out_shape=jax.ShapeDtypeStruct((TOK, 2 * LAT...]
where the time goes in v3:
time: 88.1 us; the launch traced here: 87.7 us
  Pallas kernels  84.9 us (96%)
  local copies, waits for them, and re-layouts  1.5 us (2%)
  between operations  1.29 us (1%)
    pallas_call x1, Pallas kernels, fused(): pl.pallas_call(fused_kernel, out_shape=jax.ShapeDtypeStruct((TOK, 2 * LAT...  84.9 us

profile of v3, /device:TPU:7, one launch (start us, length us, event | category | flops | bytes accessed | tf_op | source)
XLA Modules:
  0.0 87.7 jit_solution(10834612816992832434)
XLA Ops:
  1.3 84.9 %fused.1 = f32[48,128]{1,0:T(8,128)} custom-call(bf16[48,2048]{1,0:T(8,128)(2,1)} %bitcast.12, bf16[48,2048]{1,0:T(8,128)(2,1)} %bitcast.13, bf16[48,2048]{1,0:T(8,128)(2,1)} %bitcast.14, bf16[48,3072]{1,0:T(8,128)(2,1)} %bitcast.11, bf16[64,3072]{1,0:T(8,128)(2,1)} %w_ref.1, s32[1]{0:T(128)S(6)} %copy.12.step_ref, bf16[256,9216]{1,0:T(8,128)(2,1)} %mod_ref.1, ...), custom_call_target="tpu_custom_call" | custom-call | tf_op jit(solution)/shard_map/fused/pallas_call | solution.py:664
  86.2 1.5 %slice_bitcast_fusion = (f32[1,48,64]{2,1,0:T(8,128)}, f32[1,48,64]{2,1,0:T(8,128)}) fusion(f32[48,128]{1,0:T(8,128)} %fused.1), kind=kLoop, calls=%fused_computation | loop fusion | bytes 49152 | tf_op jit(solution)/shard_map/broadcast_in_dim | solution.py:747

commit v4 on v3

--- a/solution.py
+++ b/solution.py
@@ -44,27 +44,36 @@
     pltpu.make_async_copy(ref, ref, sem).wait()
 
 
-def attend(i, keys, values, q_buf, acc, peak):
-    count = keys.shape[0]
-    query = q_buf[:, i].reshape(NY * 2 * TOK, DH)
-    extended = jnp.concatenate([values, jnp.ones_like(values)], axis=1)
-    for part in range(3):
-        rows = slice(part * 128, part * 128 + 128)
-        scores = (
-            lax.dot_general(
-                query[rows], keys, (((1,), (1,)), ((), ())), preferred_element_type=jnp.float32
+def attend(tasks, q_buf, acc, peak):
+    scores = [
+        lax.dot_general(
+            q_buf[:, i].reshape(NY * ROWS, DH),
+            keys,
+            (((1,), (1,)), ((), ())),
+            preferred_element_type=jnp.float32,
+        )
+        for i, keys, _ in tasks
+    ]
+    for (i, _, values), block in zip(tasks, scores):
+        extended = jnp.concatenate([values, jnp.ones_like(values)], axis=1)
+        weights, factors = [], []
+        for part in range(3):
+            rows = slice(part * 128, part * 128 + 128)
+            piece = block[rows] * SCALE
+            old = peak[i, rows, :]
+            new = jnp.maximum(old, jnp.max(piece, axis=1, keepdims=True))
+            peak[i, rows, :] = new
+            factors.append(jnp.exp2(old - new))
+            wide = jnp.concatenate([new] * (piece.shape[1] // 128), axis=1)
+            weights.append(jnp.exp2(piece - wide).astype(jnp.bfloat16))
+        mixed = jnp.dot(
+            jnp.concatenate(weights, axis=0), extended, preferred_element_type=jnp.float32
+        )
+        for part, factor in enumerate(factors):
+            rows = slice(part * 128, part * 128 + 128)
+            acc[i, rows, :] = (
+                acc[i, rows, :] * jnp.concatenate([factor, factor], axis=1) + mixed[rows]
             )
-            * SCALE
-        )
-        old = peak[i, rows, :]
-        new = jnp.maximum(old, jnp.max(scores, axis=1, keepdims=True))
-        factor = jnp.exp2(old - new)
-        weights = jnp.exp2(scores - jnp.concatenate([new] * (count // 128), axis=1))
-        mixed = jnp.dot(
-            weights.astype(jnp.bfloat16), extended, preferred_element_type=jnp.float32
-        )
-        acc[i, rows, :] = acc[i, rows, :] * jnp.concatenate([factor, factor], axis=1) + mixed
-        peak[i, rows, :] = new
 
 
 def fused_kernel(
@@ -175,8 +184,6 @@
 
         lax.fori_loop(1, 16, send, 0)
 
-    by_head(0, k_ref, k_buf.at[queue, z], recv_k.at[c], x)
-    pltpu.make_async_copy(columns(k_ref, own_head), k_buf.at[queue, z], recv_k.at[c]).start()
     by_head(1, q_ref, q_buf.at[y, queue, zk], recv_q.at[0], xt)
 
     @pl.when(xt != x)
@@ -195,9 +202,8 @@
             columns(q_ref, own_head), q_buf.at[y, queue, zk], recv_q.at[0]
         ).start()
 
-    by_head(2, v_ref, v_buf.at[queue, z], recv_v.at[c], x)
-    pltpu.make_async_copy(columns(v_ref, own_head), v_buf.at[queue, z], recv_v.at[c]).start()
-
+    by_head(0, k_ref, k_buf.at[queue, z], recv_k.at[c], x)
+    pltpu.make_async_copy(columns(k_ref, own_head), k_buf.at[queue, z], recv_k.at[c]).start()
     for d in (1, 2, 3):
         remote(
             w_ref.at[:, own_columns(0)],
@@ -214,23 +220,15 @@
     embed = jnp.concatenate([jnp.cos(angles), jnp.sin(angles)], axis=1)
     act_all[queue] = embed / (1.0 + jnp.exp(-embed))
 
-    def send_hidden(d, carry):
+    def send_act(d, carry):
         to = (queue + d) % NQ
         device = {"queue": to, "seq": seq}
         remote(
             act_all.at[queue], act_all.at[queue], send_h.at[1], recv_h.at[1], device
         ).start()
-        remote(
-            hid_ref.at[:, pl.ds(pl.multiple_of(to * COLS, 128), COLS)],
-            hid_all.at[queue],
-            send_h.at[0],
-            recv_h.at[0],
-            device,
-        ).start()
         return carry
 
-    lax.fori_loop(1, NQ, send_hidden, 0)
-    pltpu.make_async_copy(hid_ref.at[:, own_columns(0)], hid_all.at[queue], recv_h.at[0]).start()
+    lax.fori_loop(1, NQ, send_act, 0)
 
     @pl.when(queue < NQ - 1)
     def _():
@@ -270,15 +268,18 @@
                 place(to, c, y, z),
             ).start()
 
-    for blk in range(2):
-        wait_bytes(k_buf.at[2 * x + blk], recv_k.at[blk])
-    along_x(0, k_buf)
-
     wait_bytes(q_buf.at[y], recv_q.at[0])
     for side, to in ((0, yr), (1, yl)):
         remote(
             q_buf.at[y], q_buf.at[y], send_y.at[side, 0], recv_y.at[side, 0], place(x, c, to, z)
         ).start()
+
+    by_head(2, v_ref, v_buf.at[queue, z], recv_v.at[c], x)
+    pltpu.make_async_copy(columns(v_ref, own_head), v_buf.at[queue, z], recv_v.at[c]).start()
+
+    for blk in range(2):
+        wait_bytes(k_buf.at[2 * x + blk], recv_k.at[blk])
+    along_x(0, k_buf)
 
     for load in loads:
         load.wait()
@@ -297,16 +298,28 @@
             precision=lax.Precision.HIGHEST,
         )
 
-    relay_x(0, k_buf)
-    for blk in range(2):
-        wait_bytes(v_buf.at[2 * x + blk], recv_v.at[blk])
-    along_x(1, v_buf)
     for side, source, to in ((0, yl, yr), (1, yr, yl)):
         wait_bytes(q_buf.at[source], recv_y.at[side, 0])
         slab = q_buf.at[source, pl.ds(4 * side, 4)]
         remote(
             slab, slab, send_y.at[side, 1], recv_y.at[side, 1], place(x, c, to, z)
         ).start()
+
+    for blk in range(2):
+        wait_bytes(v_buf.at[2 * x + blk], recv_v.at[blk])
+    along_x(1, v_buf)
+    relay_x(0, k_buf)
+
+    def send_hidden(d, carry):
+        to = (queue + d) % NQ
+        remote(
+            hid_ref.at[:, pl.ds(pl.multiple_of(to * COLS, 128), COLS)],
+            hid_all.at[queue],
+            send_h.at[0],
+            recv_h.at[0],
+            {"queue": to, "seq": seq},
+        ).start()
+        return carry
 
     def ring_z(step):
         for side, to in ((0, zr), (1, zl)):
@@ -378,6 +391,10 @@
         @pl.when(st == 2)
         def _():
             ring_z(1)
+            lax.fori_loop(1, NQ, send_hidden, 0)
+            pltpu.make_async_copy(
+                hid_ref.at[:, own_columns(0)], hid_all.at[queue], recv_h.at[0]
+            ).start()
             for ref, array in ((k_buf, 0), (v_buf, 1)):
                 wait_bytes(ref.at[2 * xl + 1], recv_x.at[array, 0, 1])
 
@@ -389,24 +406,26 @@
 
         high, odd = p // 2, p % 2
 
-        def both(i, carry):
+        def both(j, carry):
             keys = k_buf[pl.ds(2 * p, 2)].reshape(2 * key_rows, DH)
             values = v_buf[pl.ds(2 * p, 2)].reshape(2 * key_rows, DH)
-            attend(i, keys, values, q_buf, acc, peak)
+            attend([(2 * j, keys, values), (2 * j + 1, keys, values)], q_buf, acc, peak)
             return carry
 
         def halves(half, carry):
             same = 1 - (high - half) * (high - half)
-            count = 4 * high * (1 - half) + (2 * odd + 1) * same
-            lax.fori_loop(4 * half, 4 * half + count, both, 0)
+            count = 2 * high * (1 - half) + odd * same
+            lax.fori_loop(2 * half, 2 * half + count, both, 0)
 
             @pl.when(high == half)
             def _():
-                last = 2 * p + 1
+                keys = k_buf[pl.ds(2 * p, 2)].reshape(2 * key_rows, DH)
+                values = v_buf[pl.ds(2 * p, 2)].reshape(2 * key_rows, DH)
                 attend(
-                    last,
-                    k_buf[last].reshape(key_rows, DH),
-                    v_buf[last].reshape(key_rows, DH),
+                    [
+                        (2 * p, keys, values),
+                        (2 * p + 1, keys[key_rows:], values[key_rows:]),
+                    ],
                     q_buf,
                     acc,
                     peak,
@@ -418,12 +437,16 @@
                 for d in (2, 1, 3):
                     partial_copy(half, d).start()
 
+                @pl.when(half == 0)
+                def _():
+                    ring_z(2)
+
             return carry
 
         return lax.fori_loop(0, 2, halves, carry)
 
     lax.fori_loop(0, 4, stage, 0)
-    ring_z(2)
+    ring_z(3)
 
     def column(vector):
         return jnp.sum(
@@ -487,6 +510,7 @@
         for d in (1, 3, 2):
             wait_bytes(o_recv.at[(y + NY - d) % NY, half], recv_o.at[half, d - 1])
         merge(half)
+    for half in range(2):
         g = first(x) + 4 * half
         wait_bytes(o_all.at[c, g], recv_z.at[half])
         for d in (2, 1, 3):
@@ -498,8 +522,6 @@
                 place((x + d) % NX, c, y, z),
             ).start()
         across(g, 4 * half).start()
-        if half == 0:
-            ring_z(3)
 
     wait_bytes(hid_all, recv_h.at[0])
     for side in range(2):

time: 88.1 us -> 77.6 us (0.88)
  Pallas kernels: 84.9 us -> 74.7 us
    pallas_call x1, Pallas kernels: 84.9 us -> 74.7 us  [fused(): pl.pallas_call(fused_kernel, out_shape=jax.ShapeDtypeStruct((TOK, 2 * LAT...]
where the time goes in v4:
time: 77.6 us; the launch traced here: 77.5 us
  Pallas kernels  74.7 us (96%)
  local copies, waits for them, and re-layouts  1.5 us (2%)
  between operations  1.29 us (2%)
    pallas_call x1, Pallas kernels, fused(): pl.pallas_call(fused_kernel, out_shape=jax.ShapeDtypeStruct((TOK, 2 * LAT...  74.7 us

profile of v4, /device:TPU:7, one launch (start us, length us, event | category | flops | bytes accessed | tf_op | source)
XLA Modules:
  0.0 77.5 jit_solution(11062559692258986900)
XLA Ops:
  1.3 74.7 %fused.1 = f32[48,128]{1,0:T(8,128)} custom-call(bf16[48,2048]{1,0:T(8,128)(2,1)} %bitcast.12, bf16[48,2048]{1,0:T(8,128)(2,1)} %bitcast.13, bf16[48,2048]{1,0:T(8,128)(2,1)} %bitcast.14, bf16[48,3072]{1,0:T(8,128)(2,1)} %bitcast.11, bf16[64,3072]{1,0:T(8,128)(2,1)} %w_ref.1, s32[1]{0:T(128)S(6)} %copy.12.step_ref, bf16[256,9216]{1,0:T(8,128)(2,1)} %mod_ref.1, ...), custom_call_target="tpu_custom_call" | custom-call | tf_op jit(solution)/shard_map/fused/pallas_call | solution.py:686
  76.0 1.5 %slice_bitcast_fusion = (f32[1,48,64]{2,1,0:T(8,128)}, f32[1,48,64]{2,1,0:T(8,128)}) fusion(f32[48,128]{1,0:T(8,128)} %fused.1), kind=kLoop, calls=%fused_computation | loop fusion | bytes 49152 | tf_op jit(solution)/shard_map/broadcast_in_dim | solution.py:769

commit v5 on v4

--- a/solution.py
+++ b/solution.py
@@ -146,12 +146,14 @@
     own_head = 2 * z + c
     barrier = pltpu.get_barrier_semaphore()
 
-    def greet(j, carry):
-        device = place((x + j // 16) % NX, (c + j % 2) % NC, y, (z + (j // 2) % 8) % NZ)
-        pl.semaphore_signal(barrier, inc=1, device_id=device, device_id_type=MESH)
-        return carry
-
-    lax.fori_loop(1, 64, greet, 0)
+    queues = [(queue + d) % NQ for d in range(NQ)]
+    seqs = [(seq + d * NY) % (NY * NZ) for d in range(NZ)]
+    for d, q2 in enumerate(queues):
+        for e, s2 in enumerate(seqs):
+            if d or e:
+                pl.semaphore_signal(
+                    barrier, inc=1, device_id={"queue": q2, "seq": s2}, device_id_type=MESH
+                )
     for d in (1, 2, 3):
         pl.semaphore_signal(
             barrier, inc=1, device_id=place(x, c, (y + d) % NY, z), device_id_type=MESH
@@ -175,15 +177,18 @@
         return ref.at[:, pl.ds(pl.multiple_of(head * DH, DH), DH)]
 
     def by_head(array, ref, target, sem, xs):
-        def send(j, carry):
-            zt, ct = (z + j // 2) % NZ, (c + j % 2) % NC
+        for n in range(1, 16):
+            zt, ct = zs[n // 2], cs[n % 2]
             remote(
-                columns(ref, 2 * zt + ct), target, send_a.at[array], sem, place(xs, ct, y, zt)
+                columns(ref, 2 * zt + ct),
+                target,
+                send_a.at[array],
+                sem,
+                {"queue": xs * NC + ct, "seq": seqs[n // 2]},
             ).start()
-            return carry
-
-        lax.fori_loop(1, 16, send, 0)
-
+
+    zs = [(z + d) % NZ for d in range(NZ)]
+    cs = [c, 1 - c]
     by_head(1, q_ref, q_buf.at[y, queue, zk], recv_q.at[0], xt)
 
     @pl.when(xt != x)
@@ -220,15 +225,14 @@
     embed = jnp.concatenate([jnp.cos(angles), jnp.sin(angles)], axis=1)
     act_all[queue] = embed / (1.0 + jnp.exp(-embed))
 
-    def send_act(d, carry):
-        to = (queue + d) % NQ
-        device = {"queue": to, "seq": seq}
+    for to in queues[1:]:
         remote(
-            act_all.at[queue], act_all.at[queue], send_h.at[1], recv_h.at[1], device
+            act_all.at[queue],
+            act_all.at[queue],
+            send_h.at[1],
+            recv_h.at[1],
+            {"queue": to, "seq": seq},
         ).start()
-        return carry
-
-    lax.fori_loop(1, NQ, send_act, 0)
 
     @pl.when(queue < NQ - 1)
     def _():
@@ -475,6 +479,8 @@
                 ],
             )
             merged[g] = (mixed / total).astype(jnp.bfloat16).reshape(2, TOK, DH)
+        for k in range(4):
+            g = 4 * half + k
             for n in range(2):
                 zt = (x + 8 - g) % 4 + 4 * n
 
@@ -551,12 +557,12 @@
             g = first((x + NX - d) % NX) + 4 * half
             wait_bytes(o_all.at[c, g], recv_g.at[half, d - 1])
             across(g, 4 * half + d).start()
-        for d in range(NX):
-            g = first((x + NX - d) % NX) + 4 * half
-            wait_bytes(o_all.at[1 - c, g], recv_c.at[4 * half + d])
-
         projected = None
-        for parity in range(NC):
+        for parity in (c, 1 - c):
+            if projected is not None:
+                for d in range(NX):
+                    g = first((x + NX - d) % NX) + 4 * half
+                    wait_bytes(o_all.at[parity, g], recv_c.at[4 * half + d])
             for zh in range(0, NZ, 2):
                 left = jnp.concatenate(
                     [
@@ -593,6 +599,7 @@
                 as_row(center),
                 jnp.where(last_row == 1, as_row(spread), both_sums),
             )
+        for g in range(4 * half, 4 * half + 4):
             for later in range(2 if g < NQ - 1 else 1):
 
                 @pl.when(queue != g + later)

time: 77.6 us -> 76.3 us (0.983)
  Pallas kernels: 74.7 us -> 73.3 us
    pallas_call x1, Pallas kernels: 74.7 us -> 73.3 us  [fused(): pl.pallas_call(fused_kernel, out_shape=jax.ShapeDtypeStruct((TOK, 2 * LAT...]
where the time goes in v5:
time: 76.3 us; the launch traced here: 76.1 us
  Pallas kernels  73.3 us (96%)
  local copies, waits for them, and re-layouts  1.5 us (2%)
  between operations  1.29 us (2%)
    pallas_call x1, Pallas kernels, fused(): pl.pallas_call(fused_kernel, out_shape=jax.ShapeDtypeStruct((TOK, 2 * LAT...  73.3 us

profile of v5, /device:TPU:7, one launch (start us, length us, event | category | flops | bytes accessed | tf_op | source)
XLA Modules:
  0.0 76.1 jit_solution(16325504230510681389)
XLA Ops:
  1.3 73.3 %fused.1 = f32[48,128]{1,0:T(8,128)} custom-call(bf16[48,2048]{1,0:T(8,128)(2,1)} %bitcast.12, bf16[48,2048]{1,0:T(8,128)(2,1)} %bitcast.13, bf16[48,2048]{1,0:T(8,128)(2,1)} %bitcast.14, bf16[48,3072]{1,0:T(8,128)(2,1)} %bitcast.11, bf16[64,3072]{1,0:T(8,128)(2,1)} %w_ref.1, s32[1]{0:T(128)S(6)} %copy.12.step_ref, bf16[256,9216]{1,0:T(8,128)(2,1)} %mod_ref.1, ...), custom_call_target="tpu_custom_call" | custom-call | tf_op jit(solution)/shard_map/fused/pallas_call | solution.py:693
  74.6 1.5 %slice_bitcast_fusion = (f32[1,48,64]{2,1,0:T(8,128)}, f32[1,48,64]{2,1,0:T(8,128)}) fusion(f32[48,128]{1,0:T(8,128)} %fused.1), kind=kLoop, calls=%fused_computation | loop fusion | bytes 49152 | tf_op jit(solution)/shard_map/broadcast_in_dim | solution.py:776

commit v6 on v5

--- a/solution.py
+++ b/solution.py
@@ -395,10 +395,6 @@
         @pl.when(st == 2)
         def _():
             ring_z(1)
-            lax.fori_loop(1, NQ, send_hidden, 0)
-            pltpu.make_async_copy(
-                hid_ref.at[:, own_columns(0)], hid_all.at[queue], recv_h.at[0]
-            ).start()
             for ref, array in ((k_buf, 0), (v_buf, 1)):
                 wait_bytes(ref.at[2 * xl + 1], recv_x.at[array, 0, 1])
 
@@ -407,6 +403,10 @@
             for ref, array in ((k_buf, 0), (v_buf, 1)):
                 for side in range(2):
                     wait_bytes(ref.at[2 * x2 + side], recv_x.at[array, side, 2])
+            lax.fori_loop(1, NQ, send_hidden, 0)
+            pltpu.make_async_copy(
+                hid_ref.at[:, own_columns(0)], hid_all.at[queue], recv_h.at[0]
+            ).start()
 
         high, odd = p // 2, p % 2
 
@@ -692,7 +692,7 @@
     in_specs[5] = pl.BlockSpec(memory_space=pltpu.SMEM)
     return pl.pallas_call(
         fused_kernel,
-        out_shape=jax.ShapeDtypeStruct((TOK, 2 * LAT), f32),
+        out_shape=pltpu.VMEM((TOK, 2 * LAT), f32),
         in_specs=in_specs,
         out_specs=pl.BlockSpec(memory_space=pltpu.VMEM),
         scratch_shapes=[

time: 76.3 us -> 74.4 us (0.975)
  Pallas kernels: 73.3 us -> 72.1 us
  local copies, waits for them, and re-layouts: 1.5 us -> 0.69 us
    pallas_call x1, Pallas kernels: 73.3 us -> 72.1 us  [fused(): pl.pallas_call(fused_kernel, out_shape=pltpu.VMEM((TOK, 2 * LAT), f32), i...]
    broadcast_in_dim x1, local copies, waits for them, and re-layouts: 1.5 us -> 0.69 us  [body(): return (result[None, :, :LAT], result[None, :, LAT:])]
where the time goes in v6:
time: 74.4 us; the launch traced here: 74.1 us
  Pallas kernels  72.1 us (97%)
  between operations  1.29 us (2%)
    pallas_call x1, Pallas kernels, fused(): pl.pallas_call(fused_kernel, out_shape=pltpu.VMEM((TOK, 2 * LAT), f32), i...  72.1 us

profile of v6, /device:TPU:7, one launch (start us, length us, event | category | flops | bytes accessed | tf_op | source)
XLA Modules:
  0.0 74.1 jit_solution(9884110303942702478)
XLA Ops:
  1.3 72.1 %fused.1 = f32[48,128]{1,0:T(8,128)S(1)} custom-call(bf16[48,2048]{1,0:T(8,128)(2,1)} %bitcast.12, bf16[48,2048]{1,0:T(8,128)(2,1)} %bitcast.13, bf16[48,2048]{1,0:T(8,128)(2,1)} %bitcast.14, bf16[48,3072]{1,0:T(8,128)(2,1)} %bitcast.11, bf16[64,3072]{1,0:T(8,128)(2,1)} %w_ref.1, s32[1]{0:T(128)S(6)} %copy.12.step_ref, bf16[256,9216]{1,0:T(8,128)(2,1)} %mod_ref.1, ...), custom_call_target="tpu_custom_call" | custom-call | tf_op jit(solution)/shard_map/fused/pallas_call | solution.py:693
  73.4 0.7 slice_bitcast_fusion

commit v7 on v6

--- a/solution.py
+++ b/solution.py
@@ -273,10 +273,13 @@
             ).start()
 
     wait_bytes(q_buf.at[y], recv_q.at[0])
-    for side, to in ((0, yr), (1, yl)):
-        remote(
-            q_buf.at[y], q_buf.at[y], send_y.at[side, 0], recv_y.at[side, 0], place(x, c, to, z)
-        ).start()
+    for n in range(2):
+        for side, to in ((0, yr), (1, yl)):
+            part = n if side == 0 else 1 - n
+            slab = q_buf.at[y, pl.ds(4 * part, 4)]
+            remote(
+                slab, slab, send_y.at[side, part], recv_y.at[side, part], place(x, c, to, z)
+            ).start()
 
     by_head(2, v_ref, v_buf.at[queue, z], recv_v.at[c], x)
     pltpu.make_async_copy(columns(v_ref, own_head), v_buf.at[queue, z], recv_v.at[c]).start()
@@ -303,10 +306,10 @@
         )
 
     for side, source, to in ((0, yl, yr), (1, yr, yl)):
-        wait_bytes(q_buf.at[source], recv_y.at[side, 0])
         slab = q_buf.at[source, pl.ds(4 * side, 4)]
+        wait_bytes(slab, recv_y.at[side, side])
         remote(
-            slab, slab, send_y.at[side, 1], recv_y.at[side, 1], place(x, c, to, z)
+            slab, slab, send_y.at[side, 2], recv_y.at[side, 2], place(x, c, to, z)
         ).start()
 
     for blk in range(2):
@@ -343,8 +346,9 @@
 
     wait_bytes(w_all.at[z], recv_wy.at[0])
     ring_z(0)
-    for side in range(2):
-        wait_bytes(q_buf.at[y2, pl.ds(4 * side, 4)], recv_y.at[side, 1])
+    for side, source in ((0, yl), (1, yr)):
+        wait_bytes(q_buf.at[source, pl.ds(4 - 4 * side, 4)], recv_y.at[side, 1 - side])
+        wait_bytes(q_buf.at[y2, pl.ds(4 * side, 4)], recv_y.at[side, 2])
 
     lane = lax.broadcasted_iota(jnp.int32, (ROWS, 128), 1)
     row = lax.broadcasted_iota(jnp.int32, (ROWS, 128), 0)
@@ -441,16 +445,12 @@
                 for d in (2, 1, 3):
                     partial_copy(half, d).start()
 
-                @pl.when(half == 0)
-                def _():
-                    ring_z(2)
-
             return carry
 
         return lax.fori_loop(0, 2, halves, carry)
 
     lax.fori_loop(0, 4, stage, 0)
-    ring_z(3)
+    ring_z(2)
 
     def column(vector):
         return jnp.sum(
@@ -529,6 +529,7 @@
             ).start()
         across(g, 4 * half).start()
 
+    ring_z(3)
     wait_bytes(hid_all, recv_h.at[0])
     for side in range(2):
         wait_bytes(w_all.at[(z + 4) % NZ, pl.ds(2 * side, 2)], recv_wz.at[side, 3])
@@ -654,8 +655,8 @@
         for array in range(2):
             for n in range(3):
                 wait_bytes(k_buf.at[0], send_x.at[array, side, n])
-        wait_bytes(q_buf.at[0], send_y.at[side, 0])
-        wait_bytes(q_buf.at[0, pl.ds(0, 4)], send_y.at[side, 1])
+        for n in range(3):
+            wait_bytes(q_buf.at[0, pl.ds(0, 4)], send_y.at[side, n])
         for step in range(4):
             wait_bytes(w_all.at[0, pl.ds(0, NY if step < 3 else 2)], send_wz.at[side, step])
     for d in (1, 2, 3):
@@ -722,7 +723,7 @@
             dma((3,)),
             dma((2, 4)),
             dma((2, 2, 3)),
-            dma((2, 2)),
+            dma((2, 3)),
             dma((2, 3)),
             dma((1,)),
             dma((2, 3)),
@@ -735,7 +736,7 @@
             dma((1,)),
             dma((2, 4)),
             dma((2, 2, 3)),
-            dma((2, 2)),
+            dma((2, 3)),
             dma((2, 3)),
             dma((2,)),
             dma((2, 3)),

time: 74.4 us -> 74.7 us (level)
  no operation moved by 1% of the time
where the time goes in v7:
time: 74.7 us; the launch traced here: 74.6 us
  Pallas kernels  72.7 us (97%)
  between operations  1.29 us (2%)
    pallas_call x1, Pallas kernels, fused(): pl.pallas_call(fused_kernel, out_shape=pltpu.VMEM((TOK, 2 * LAT), f32), i...  72.7 us

profile of v7, /device:TPU:7, one launch (start us, length us, event | category | flops | bytes accessed | tf_op | source)
XLA Modules:
  0.0 74.6 jit_solution(18216771705318031381)
XLA Ops:
  1.3 72.7 %fused.1 = f32[48,128]{1,0:T(8,128)S(1)} custom-call(bf16[48,2048]{1,0:T(8,128)(2,1)} %bitcast.12, bf16[48,2048]{1,0:T(8,128)(2,1)} %bitcast.13, bf16[48,2048]{1,0:T(8,128)(2,1)} %bitcast.14, bf16[48,3072]{1,0:T(8,128)(2,1)} %bitcast.11, bf16[64,3072]{1,0:T(8,128)(2,1)} %w_ref.1, s32[1]{0:T(128)S(6)} %copy.12.step_ref, bf16[256,9216]{1,0:T(8,128)(2,1)} %mod_ref.1, ...), custom_call_target="tpu_custom_call" | custom-call | tf_op jit(solution)/shard_map/fused/pallas_call | solution.py:694
  73.9 0.7 slice_bitcast_fusion
